TPU v7x, 32 devices: a whole 2x2x4 slice. The times are simulated.
32 devices in a mesh: row: 4 (over z), col: 8 (over y, x, core).
Axes of the slice: x: 2, y: 2, z: 4, core: 2. Of those that a mesh axis runs over, the one named last changes fastest.
Arguments:
- hidden_input: bfloat16 [4096, 1536], P(('row', 'col')), may hold values from -6 to 6
- lengths: int32 [4, 4], replicated, may hold values from 1 to 768, 1024 in all within a row
- prompt_adapter: int32 [4, 4], replicated, may hold values from 0 to 31
- routes: int32 [4096, 4], P(('row', 'col')), may hold values from 0 to 15, all different within a row; in each aligned block of 128 rows (0 to 127, 128 to 255, ...) at most 40 rows name the same one
- attention_norm_gain: bfloat16 [1536], replicated, may hold values from 0.5 to 1.5
- expert_norm_gain: bfloat16 [1536], replicated, may hold values from 0.5 to 1.5
- projection_weight: bfloat16 [1536, 2048], P('row', 'col')
- output_weight: bfloat16 [1536, 1536], P('row', 'col'), may hold values from -0.15625 to 0.15625
- router: bfloat16 [1536, 16], replicated, may hold values from -0.5 to 0.5
- adapter_projection_down: bfloat16 [32, 16, 1536], P('col'), may hold values from -0.15625 to 0.15625
- adapter_projection_up: bfloat16 [32, 16, 2048], P('col'), may hold values from -1.5 to 1.5
- adapter_output_down: bfloat16 [32, 16, 1536], P('col'), may hold values from -0.15625 to 0.15625
- adapter_output_up: bfloat16 [32, 16, 1536], P('col'), may hold values from -1.5 to 1.5
- expert_gate_weight: bfloat16 [16, 1536, 768], P('col'), may hold values from -0.15625 to 0.15625
- expert_up_weight: bfloat16 [16, 1536, 768], P('col'), may hold values from -0.15625 to 0.15625
- expert_down_weight: bfloat16 [16, 768, 1536], P('col'), may hold values from -0.21875 to 0.21875
Outputs:
- hidden_out: bfloat16 [4096, 1536], P(('row', 'col'))
Inputs may be any that keep to these rules, and one draw needn't show every extreme that they name: The 4 lengths of a block sum to 1024; in every block the longest prompt has exactly 768 tokens. `prompt_adapter`: adapter a is held by index a // 4 of col. `routes`: the 4 experts of a token differ; among the rows of one device no expert is named more than 40 times, a bound that some block reaches. Expert e is held by index e // 2 of col.
All inputs are finite; a program needn't handle non-finite values.
Results may differ from a plain program's by a relative error of at most 0.012.
Values may be sent and summed in bfloat16 or wider, within the bound.
A program may use at most 128 MiB of HBM per device.

v0:
```python
import jax
import jax.numpy as jnp
from jax import lax
from jax.sharding import PartitionSpec as P

QUERY_HEADS = 12
KEY_HEADS = 2
HEAD_SIZE = 128
QUERY_PER_KEY = 6
CAP = 40


norm_eps = 1e-06
rope_base = 1000000.0
adapter_scale = 0.5


def rms_scaled(value_tensor, norm_gain):
    widened = value_tensor.astype(jnp.float32)
    inverse = lax.rsqrt(jnp.mean(widened * widened, axis=-1, keepdims=True) + norm_eps)
    return (widened * inverse * norm_gain.astype(jnp.float32)).astype(jnp.bfloat16)


def prompt_layout(lengths_row, tok_index):
    prompt_ends = jnp.cumsum(lengths_row)
    starts = prompt_ends - lengths_row
    prompt_of = jnp.sum((tok_index[:, None] >= prompt_ends[None, :]).astype(jnp.int32), axis=1)
    within_prompt = prompt_of[:, None] == jnp.arange(lengths_row.shape[0], dtype=jnp.int32)[None, :]
    token_positions = tok_index - jnp.sum(jnp.where(within_prompt, starts[None, :], 0), axis=1)
    return (prompt_of, within_prompt, token_positions)


def apply_rotary(value_tensor, token_positions):
    half_width = value_tensor.shape[-1] // 2
    frequency = rope_base ** (
        -2.0 * jnp.arange(half_width, dtype=jnp.float32) / value_tensor.shape[-1]
    )
    angles = token_positions.astype(jnp.float32)[:, None] * frequency[None, :]
    cosine = jnp.cos(angles)[:, None, :]
    sine_part = jnp.sin(angles)[:, None, :]
    front_half = value_tensor[..., :half_width]
    back_half = value_tensor[..., half_width:]
    return jnp.concatenate(
        [front_half * cosine - back_half * sine_part, back_half * cosine + front_half * sine_part],
        axis=-1,
    )


def adapter_change(inputs, within_prompt, downs, ups):
    low_rank = jnp.einsum("nk,prk->npr", inputs, downs, preferred_element_type=jnp.float32)
    low_rank = jnp.where(within_prompt[:, :, None], low_rank, 0.0).astype(jnp.bfloat16)
    return jnp.einsum("npr,pro->no", low_rank, ups, preferred_element_type=jnp.float32)


def route_slots(flat_routes, expert_total):
    marks = (flat_routes[:, None] == jnp.arange(expert_total, dtype=jnp.int32)[None, :]).astype(
        jnp.int32
    )
    before = jnp.cumsum(marks, axis=0) - marks
    return jnp.sum(before * marks, axis=1)


def local(
    hidden_input,
    lengths,
    prompt_adapter,
    routes,
    attention_norm_gain,
    expert_norm_gain,
    projection_weight,
    output_weight,
    router,
    adapter_projection_down,
    adapter_projection_up,
    adapter_output_down,
    adapter_output_up,
    expert_gate_weight,
    expert_up_weight,
    expert_down_weight,
):
    token_rows = hidden_input.shape[0]
    model_width = hidden_input.shape[1]
    columns = lax.axis_size("col")
    row_index = lax.axis_index("row")
    col_index = lax.axis_index("col")
    lengths_row = lax.dynamic_index_in_dim(lengths, row_index, 0, keepdims=False)
    adapter_row = lax.dynamic_index_in_dim(prompt_adapter, row_index, 0, keepdims=False)
    tok_index = col_index * token_rows + jnp.arange(token_rows, dtype=jnp.int32)
    prompt_of, within_prompt, token_positions = prompt_layout(lengths_row, tok_index)
    wide_parts = (
        lax.all_gather(projection_weight, "col", axis=1, tiled=True),
        lax.all_gather(output_weight, "col", axis=1, tiled=True),
    )
    qkv_full, out_full = (
        lax.all_gather(wide_parts[0], "row", axis=0, tiled=True),
        lax.all_gather(wide_parts[1], "row", axis=0, tiled=True),
    )
    owner_column = adapter_row // adapter_projection_down.shape[0]
    nearby_slot = adapter_row % adapter_projection_down.shape[0]
    owned_here = (owner_column == col_index)[:, None, None]

    def choose_experts(table):
        return jnp.where(owned_here, jnp.take(table, nearby_slot, axis=0).astype(jnp.float32), 0.0)

    summed = (
        lax.psum(choose_experts(adapter_projection_down).astype(jnp.bfloat16), "col").astype(
            jnp.float32
        ),
        lax.psum(choose_experts(adapter_projection_up).astype(jnp.bfloat16), "col").astype(
            jnp.float32
        ),
        lax.psum(choose_experts(adapter_output_down).astype(jnp.bfloat16), "col").astype(
            jnp.float32
        ),
        lax.psum(choose_experts(adapter_output_up).astype(jnp.bfloat16), "col").astype(jnp.float32),
    )
    projection_down_map = summed[0].astype(jnp.bfloat16)
    projection_up_map = summed[1].astype(jnp.bfloat16)
    output_down_map = summed[2].astype(jnp.bfloat16)
    output_up_map = summed[3].astype(jnp.bfloat16)
    normalized = rms_scaled(hidden_input, attention_norm_gain)
    projection_all = jnp.dot(normalized, qkv_full, preferred_element_type=jnp.float32)
    projection_all = projection_all + adapter_scale * adapter_change(
        normalized, within_prompt, projection_down_map, projection_up_map
    )
    query_slice = apply_rotary(
        projection_all[:, : QUERY_HEADS * HEAD_SIZE].reshape(token_rows, QUERY_HEADS, HEAD_SIZE),
        token_positions,
    ).astype(jnp.bfloat16)
    key_slice = apply_rotary(
        projection_all[:, QUERY_HEADS * HEAD_SIZE : (QUERY_HEADS + KEY_HEADS) * HEAD_SIZE].reshape(
            token_rows, KEY_HEADS, HEAD_SIZE
        ),
        token_positions,
    ).astype(jnp.bfloat16)
    value_slice = projection_all[:, (QUERY_HEADS + KEY_HEADS) * HEAD_SIZE :].astype(jnp.bfloat16)
    flattened_keys = key_slice.reshape(token_rows, KEY_HEADS * HEAD_SIZE)
    grouped = (
        query_slice.reshape(token_rows, KEY_HEADS, QUERY_PER_KEY, HEAD_SIZE)
        .transpose(1, 2, 0, 3)
        .reshape(KEY_HEADS, QUERY_PER_KEY * token_rows, HEAD_SIZE)
    )
    query_index = jnp.tile(tok_index, QUERY_PER_KEY)
    query_prompt = jnp.tile(prompt_of, QUERY_PER_KEY)
    segments = (
        lax.all_gather(flattened_keys, "col", axis=0, tiled=True),
        lax.all_gather(value_slice, "col", axis=0, tiled=True),
    )
    best_experts = jnp.full((KEY_HEADS, QUERY_PER_KEY * token_rows), -1e30, jnp.float32)
    segment_length = segments[0].shape[0]
    key_lines = segments[0].reshape(segment_length, KEY_HEADS, HEAD_SIZE).transpose(1, 0, 2)
    value_lines = segments[1].reshape(segment_length, KEY_HEADS, HEAD_SIZE).transpose(1, 0, 2)
    key_index = jnp.arange(segment_length, dtype=jnp.int32)
    key_prompt = prompt_layout(lengths_row, key_index)[0]
    allowed = (key_prompt[None, :] == query_prompt[:, None]) & (
        key_index[None, :] <= query_index[:, None]
    )
    scores = jnp.einsum(
        "hqd,hkd->hqk", grouped, key_lines, preferred_element_type=jnp.float32
    ) * HEAD_SIZE ** (-0.5)
    masked = jnp.where(allowed[None], scores, -1e30)
    fresh = jnp.maximum(best_experts, jnp.max(masked, axis=-1))
    weights = jnp.where(allowed[None], jnp.exp(scores - fresh[..., None]), 0.0)
    running_new = jnp.sum(weights, axis=-1)
    accum_new = jnp.einsum(
        "hqk,hkd->hqd",
        weights.astype(jnp.bfloat16),
        value_lines,
        preferred_element_type=jnp.float32,
    )
    mixed_output = accum_new / running_new[..., None]
    attention_result = (
        mixed_output.reshape(KEY_HEADS, QUERY_PER_KEY, token_rows, HEAD_SIZE)
        .transpose(2, 0, 1, 3)
        .reshape(token_rows, QUERY_HEADS * HEAD_SIZE)
        .astype(jnp.bfloat16)
    )
    projected_rows = jnp.dot(attention_result, out_full, preferred_element_type=jnp.float32)
    projected_rows = projected_rows + adapter_scale * adapter_change(
        attention_result, within_prompt, output_down_map, output_up_map
    )
    residual = (hidden_input.astype(jnp.float32) + projected_rows).astype(jnp.bfloat16)
    normed_two = rms_scaled(residual, expert_norm_gain)
    logits = jnp.dot(normed_two, router, preferred_element_type=jnp.float32)
    squashed = jax.nn.sigmoid(jnp.take_along_axis(logits, routes, axis=1))
    mixing = squashed / jnp.sum(squashed, axis=1, keepdims=True)
    expert_total = router.shape[1]
    local_experts = expert_gate_weight.shape[0]
    flat_routes = routes.reshape(-1)
    slots = route_slots(flat_routes, expert_total)
    token_of = jnp.arange(flat_routes.shape[0], dtype=jnp.int32) // routes.shape[1]
    dispatch_rows = (
        jnp.zeros((expert_total, CAP, model_width), jnp.bfloat16)
        .at[flat_routes, slots]
        .set(normed_two[token_of])
    )
    sending = dispatch_rows.reshape(columns, local_experts, CAP, model_width)
    arrived = lax.all_to_all(sending, "col", split_axis=0, concat_axis=0, tiled=True)
    gate_vals = jnp.einsum(
        "sjcd,jdf->sjcf", arrived, expert_gate_weight, preferred_element_type=jnp.float32
    )
    up_vals = jnp.einsum(
        "sjcd,jdf->sjcf", arrived, expert_up_weight, preferred_element_type=jnp.float32
    )
    hidden_vals = (jnp.maximum(gate_vals, 0.0) * up_vals).astype(jnp.bfloat16)
    answered = jnp.einsum(
        "sjcf,jfd->sjcd", hidden_vals, expert_down_weight, preferred_element_type=jnp.float32
    ).astype(jnp.bfloat16)
    returned = lax.all_to_all(answered, "col", split_axis=0, concat_axis=0, tiled=True)
    results = returned.reshape(expert_total, CAP, model_width)[flat_routes, slots]
    combined = jnp.sum(
        results.astype(jnp.float32).reshape(token_rows, routes.shape[1], model_width)
        * mixing[:, :, None],
        axis=1,
    )
    return (residual.astype(jnp.float32) + combined).astype(jnp.bfloat16)


def solution(mesh):
    placed = (
        P(("row", "col"), None),
        P(),
        P(),
        P(("row", "col"), None),
        P(),
        P(),
        P("row", "col"),
        P("row", "col"),
        P(),
        P("col", None, None),
        P("col", None, None),
        P("col", None, None),
        P("col", None, None),
        P("col", None, None),
        P("col", None, None),
        P("col", None, None),
    )
    return jax.shard_map(
        local, mesh=mesh, in_specs=placed, out_specs=P(("row", "col"), None), check_vma=False
    )
```

profile of v0, /device:TPU:1, one launch (start us, length us, event | category | flops | bytes accessed | tf_op | source)
XLA Modules:
  0.0 487.4 jit_solution(2084472172162816337)
XLA Ops:
  8.1 29.6 %all-gather.5.cloned.1.call-done = bf16[384,2048]{1,0:T(8,128)(2,1)} async-done(((bf16[384,256]{1,0:T(8,128)(2,1)}), bf16[384,2048]{1,0:T(8,128)(2,1)}) %all-gather.5.cloned.1.call-update) | async-done | bytes 1572880 | tf_op jit(solution)/shard_map/all_gather | solution.py:91
  46.8 16.8 %all-gather.9.cloned.1.call-done = bf16[384,1536]{0,1:T(8,128)(2,1)} async-done(((bf16[384,192]{0,1:T(8,128)(2,1)}), bf16[384,1536]{0,1:T(8,128)(2,1)}) %all-gather.9.cloned.1.call-update) | async-done | bytes 1179664 | tf_op jit(solution)/shard_map/all_gather | solution.py:92
  68.2 112.2 %all-gather.7.cloned.1.call-done = bf16[1536,2048]{1,0:T(8,128)(2,1)} async-done(((bf16[384,2048]{1,0:T(8,128)(2,1)}), bf16[1536,2048]{1,0:T(8,128)(2,1)}) %all-gather.7.cloned.1.call-update) | async-done | bytes 6291472 | tf_op jit(solution)/shard_map/all_gather | solution.py:95
  180.4 3.8 fusion.57
  184.2 53.0 %all-reduce.3.cloned.1.call-done = (bf16[4,16,1536]{2,1,0:T(8,128)(2,1)}, bf16[4,16,2048]{2,1,0:T(8,128)(2,1)}, bf16[4,16,1536]{2,1,0:T(8,128)(2,1)}, bf16[4,16,1536]{2,1,0:T(8,128)(2,1)}) async-done(((bf16[4,16,1536]{2,1,0:T(8,128)(2,1)}, bf16[4,16,2048]{2,1,0:T(8,128)(2,1)}, bf16[4,16,1536]{2,1,0:T(8,128)(2,1)}, bf16[4,16,1536]{2,1,0:T(8,128)(2,1)}), (bf16[4,16,1536]{2,1,0:T(8,128)(2,1)}, ...) | async-done | bytes 851984 | tf_op jit(solution)/shard_map/psum | solution.py:115
  237.2 1.9 fusion.21
  241.4 10.6 %all_gather.20 = bf16[1024,256]{0,1:T(8,128)(2,1)S(1)} all-gather(bf16[128,256]{0,1:T(8,128)(2,1)S(1)} %bitcast.157), channel_id=1, replica_groups=mesh['row'=4,'col'=8] {'col'}, dimensions={0}, use_global_device_ids=true | all-gather | bytes 589824 | tf_op jit(solution)/shard_map/all_gather | solution.py:146
  253.6 9.8 %all_gather.21 = bf16[1024,256]{1,0:T(8,128)(2,1)S(1)} all-gather(bf16[128,256]{1,0:T(8,128)(2,1)} %slice.71), channel_id=1, replica_groups=mesh['row'=4,'col'=8] {'col'}, dimensions={0}, use_global_device_ids=true | all-gather | bytes 589824 | tf_op jit(solution)/shard_map/all_gather | solution.py:147
  263.5 1.5 select_reduce_fusion
  265.0 2.2 fusion
  267.2 1.6 fusion.40
  269.6 58.7 %all-gather.11.cloned.1.call-done = bf16[1536,1536]{0,1:T(8,128)(2,1)} async-done(((bf16[384,1536]{0,1:T(8,128)(2,1)}), bf16[1536,1536]{0,1:T(8,128)(2,1)}) %all-gather.11.cloned.1.call-update) | async-done | bytes 4718608 | tf_op jit(solution)/shard_map/all_gather | solution.py:96
  328.3 4.1 multiply_reduce_fusion.1
  333.4 3.0 gather_fusion.1
  336.5 58.1 %scatter_fusion = bf16[16,40,1536]{2,1,0:T(8,128)(2,1)S(1)} fusion(bf16[16,40,1536]{2,1,0:T(8,128)(2,1)S(1)} %broadcast_in_dim.160, s32[512]{0:T(512)S(1)} %bitcast.148, bf16[512,1536]{1,0:T(8,128)(2,1)} %gather_fusion.1), kind=kCustom, calls=%fused_computation.7 | custom fusion | bytes 4722688 | tf_op jit(solution)/shard_map/scatter | solution.py:195
  394.6 28.4 %all_to_all.10 = bf16[8,2,40,1536]{3,2,1,0:T(8,128)(2,1)S(1)} all-to-all(bf16[8,2,40,1536]{3,2,1,0:T(8,128)(2,1)S(1)} %bitcast.145), channel_id=1, replica_groups=mesh['row'=4,'col'=8] {'col'}, dimensions={0} | all-to-all | bytes 3932160 | tf_op jit(solution)/shard_map/all_to_all | solution.py:198
  424.2 5.3 %fusion.4 = f32[2,8,40,768]{3,2,1,0:T(8,128)} fusion(bf16[2,1536,768]{2,1,0:T(8,128)(2,1)} %param.32, bf16[8,2,40,1536]{3,2,1,0:T(8,128)(2,1)S(1)} %all_to_all.10), kind=kOutput, calls=%fused_computation.14 | convolution fusion | flops 1509949440 | bytes 8650752 | tf_op jit(solution)/shard_map/sjcd,jdf->sjcf/dot_general | solution.py:202
  429.6 8.1 %fusion.15 = bf16[8,2,40,1536]{3,2,0,1:T(8,128)(2,1)S(1)} fusion(bf16[2,768,1536]{2,1,0:T(8,128)(2,1)} %param.33, f32[2,8,40,768]{3,2,1,0:T(8,128)} %fusion.4, bf16[2,1536,768]{2,1,0:T(8,128)(2,1)} %param.31, bf16[8,2,40,1536]{3,2,1,0:T(8,128)(2,1)} %copy-done.5), kind=kOutput, calls=%fused_computation.24 | convolution fusion | flops 3022356480 | bytes 15335424 | tf_op jit(solution)/shard_map/sjcf,jfd->sjcd/dot_general | solution.py:206
  439.2 4.4 all-to-all-start.1
  444.0 3.8 gather_fusion.3
  448.1 17.0 %all-to-all-done.1 = bf16[8,2,40,1536]{3,2,1,0:T(8,128)(2,1)S(1)} async-done(((bf16[8,2,40,1536]{3,2,1,0:T(8,128)(2,1)}), bf16[8,2,40,1536]{3,2,1,0:T(8,128)(2,1)S(1)}, u32[]{:S(2)}, u32[]{:S(2)}) %all-to-all-start.1) | async-done | bytes 1966112 | tf_op jit(solution)/shard_map/all_to_all | solution.py:209
  465.2 9.7 %gather_fusion.2 = bf16[512,1536]{1,0:T(8,128)(2,1)} fusion(bf16[16,40,1536]{2,1,0:T(8,128)(2,1)S(1)} %bitcast.146, s32[512]{0:T(512)S(1)} %bitcast.147), kind=kCustom, calls=%fused_computation.5 | custom fusion | bytes 3149824 | tf_op jit(solution)/shard_map/gather | solution.py:210
  474.9 2.9 reshape.450
  477.8 2.2 multiply_reduce_fusion
  (110 shorter events, 25.0 us)
Async XLA Ops:
  6.5 37.2 %copy-start = (bf16[4,16,2048]{2,1,0:T(8,128)(2,1)S(1)}, bf16[4,16,2048]{2,1,0:T(8,128)(2,1)}, u32[]{:S(2)}) copy-start(bf16[4,16,2048]{2,1,0:T(8,128)(2,1)} %param.28) | copy-start | bytes 786436
  6.5 39.6 %copy-start.10 = (s32[128,4]{0,1:T(4,128)S(1)}, s32[128,4]{0,1:T(4,128)}, u32[]{:S(2)}) copy-start(s32[128,4]{0,1:T(4,128)} %param.21) | copy-start | bytes 6148
  6.5 31.1 %all-gather.5.cloned.1.call-start = ((), (), s32[]{:S(2)}) async-start(), calls=%async_computation.2 | async-start | bytes 1769472 | tf_op jit(solution)/shard_map/all_gather | solution.py:91
  7.3 39.4 %copy-start.13 = (s32[4,4]{1,0:T(4,128)S(1)}, s32[4,4]{1,0:T(4,128)}, u32[]{:S(2)}) copy-start(s32[4,4]{1,0:T(4,128)} %param.19) | copy-start | bytes 196
  7.3 39.6 %copy-start.11 = (bf16[1536]{0:T(1024)(128)(2,1)S(1)}, bf16[1536]{0:T(1024)(128)(2,1)}, u32[]{:S(2)}) copy-start(bf16[1536]{0:T(1024)(128)(2,1)} %param.22) | copy-start | bytes 9220
  7.3 56.4 %all-gather.9.cloned.1.call-start = ((), (), s32[]{:S(2)}) async-start(), calls=%async_computation.4 | async-start | bytes 1327104 | tf_op jit(solution)/shard_map/all_gather | solution.py:92
  8.0 172.4 %all-gather.7.cloned.1.call-start = ((), (), s32[]{:S(2)}) async-start(), calls=%async_computation.3 | async-start | bytes 7864320 | tf_op jit(solution)/shard_map/all_gather | solution.py:95
  37.7 27.9 %copy-start.12 = (bf16[1536]{0:T(1024)(128)(2,1)S(1)}, bf16[1536]{0:T(1024)(128)(2,1)}, u32[]{:S(2)}) copy-start(bf16[1536]{0:T(1024)(128)(2,1)} %param.23) | copy-start | bytes 9220
  37.7 29.5 %copy-start.4 = (bf16[128,1536]{1,0:T(8,128)(2,1)S(1)}, bf16[128,1536]{1,0:T(8,128)(2,1)}, u32[]{:S(2)}) copy-start(bf16[128,1536]{1,0:T(8,128)(2,1)} %param.18) | copy-start | bytes 1179652
  37.7 199.5 %all-reduce.3.cloned.1.call-start = ((), (), s32[]{:S(2)}) async-start(), calls=%async_computation.6 | async-start | bytes 1703936 | tf_op jit(solution)/shard_map/psum | solution.py:115
  46.1 282.2 %all-gather.11.cloned.1.call-start = ((), (), s32[]{:S(2)}) async-start(), calls=%async_computation.5 | async-start | bytes 5898240 | tf_op jit(solution)/shard_map/all_gather | solution.py:96
  64.1 3.3 copy-start.6
  267.2 1.9 copy-start.7
  267.2 1.9 copy-start.8
  332.4 0.9 copy-start.2
  423.0 1.3 copy-start.5
  437.7 6.1 %copy-start.9 = (bf16[1536,16]{0,1:T(8,128)(2,1)S(1)}, bf16[1536,16]{0,1:T(8,128)(2,1)}, u32[]{:S(2)}) copy-start(bf16[1536,16]{0,1:T(8,128)(2,1)} %param.26) | copy-start | bytes 147460
  439.2 26.0 %all-to-all-start.1 = ((bf16[8,2,40,1536]{3,2,1,0:T(8,128)(2,1)}), bf16[8,2,40,1536]{3,2,1,0:T(8,128)(2,1)S(1)}, u32[]{:S(2)}, u32[]{:S(2)}) async-start(bf16[8,2,40,1536]{3,2,1,0:T(8,128)(2,1)} %copy.140), calls=%async_computation.1 | async-start | bytes 3932160 | tf_op jit(solution)/shard_map/all_to_all | solution.py:209
  474.9 6.0 %copy-start.1 = (bf16[4,16,2048]{2,1,0:T(8,128)(2,1)S(1)}, bf16[4,16,2048]{2,1,0:T(8,128)(2,1)}, u32[]{:S(2)}) copy-start(bf16[4,16,2048]{2,1,0:T(8,128)(2,1)} %param.28) | copy-start | bytes 786436
  477.8 2.2 copy-start.3
Sparse Core Ops, SparseCore 0:
  9.2 28.3 all-gather.4
  39.5 24.0 all-gather.8
  65.2 115.1 all-gather.6
  183.8 53.3 all-reduce.2
  238.7 89.5 all-gather.10
where the time goes:
time: 493 us; the launch traced here: 487 us
  waiting for transfers between devices  289 us (59%)
  local copies, waits for them, and re-layouts  90.7 us (18%)
  blocking collectives  48.8 us (10%)
  matrix products  27.1 us (5%)
  other arithmetic  13.8 us (3%)
  between operations  13.7 us (3%)
    all_gather x1, waiting for transfers between devices, local(): lax.all_gather(wide_parts[0], 'row', axis=0, tiled=True)  112 us
    all_gather x1, waiting for transfers between devices, local(): lax.all_gather(wide_parts[1], 'row', axis=0, tiled=True)  58.7 us
    scatter x1, local copies, waits for them, and re-layouts, local(): dispatch_rows = jnp.zeros((expert_total, CAP, model_width), jnp.bfloat16)...  58.1 us
    psum x1, waiting for transfers between devices, local(): lax.psum(choose_experts(adapter_output_up).astype(jnp.bfloat16), 'col')  53 us
    all_gather x1, waiting for transfers between devices, local(): lax.all_gather(projection_weight, 'col', axis=1, tiled=True)  29.6 us
    all_to_all x1, blocking collectives, local(): lax.all_to_all(sending, 'col', split_axis=0, concat_axis=0, tiled=True)  28.4 us
    all_to_all x1, waiting for transfers between devices, local(): lax.all_to_all(answered, 'col', split_axis=0, concat_axis=0, tiled=True)  17 us
    all_gather x1, waiting for transfers between devices, local(): lax.all_gather(output_weight, 'col', axis=1, tiled=True)  16.8 us
  transfers between devices with their start and end apart: 6, of which 6 were waited for; matrix products, arithmetic and copies ran while one was open for 7% of the time, Pallas kernels for 0%

commit v1 on v0

--- a/solution.py
+++ b/solution.py
@@ -1,6 +1,10 @@
+import functools
+
 import jax
 import jax.numpy as jnp
 from jax import lax
+from jax.experimental import pallas as pl
+from jax.experimental.pallas import tpu as pltpu
 from jax.sharding import PartitionSpec as P
 
 QUERY_HEADS = 12
@@ -58,6 +62,323 @@
     )
     before = jnp.cumsum(marks, axis=0) - marks
     return jnp.sum(before * marks, axis=1)
+
+
+def meet(peers):
+    barrier = pltpu.get_barrier_semaphore()
+    for peer in peers:
+        pl.semaphore_signal(
+            barrier, inc=1, device_id=peer, device_id_type=pl.DeviceIdType.MESH
+        )
+    pl.semaphore_wait(barrier, len(peers))
+
+
+def remote(source, target, send_sem, recv_sem, peer):
+    return pltpu.make_async_remote_copy(
+        src_ref=source,
+        dst_ref=target,
+        send_sem=send_sem,
+        recv_sem=recv_sem,
+        device_id=peer,
+        device_id_type=pl.DeviceIdType.MESH,
+    )
+
+
+def gather_kernel(
+    rows,
+    columns,
+    proj_ref,
+    out_ref,
+    maps_ref,
+    all_proj,
+    all_out,
+    all_maps,
+    parts,
+    chunk,
+    own_sem,
+    line_send,
+    line_recv,
+    plane_send,
+    plane_recv,
+    pair_send,
+    pair_recv,
+    part_send,
+    part_recv,
+    map_send,
+    map_recv,
+):
+    row = lax.axis_index("row")
+    col = lax.axis_index("col")
+    chips = columns // 2
+    core = lax.rem(col, 2)
+    chip = col // 2
+    sibling = chip * 2 + 1 - core
+    square = chips == 4
+
+    def at_row(target):
+        return {"row": target, "col": col}
+
+    def at_col(target):
+        return {"row": row, "col": target}
+
+    peers = [at_row(lax.rem(row + s, rows)) for s in range(1, rows)]
+    peers += [at_col(lax.rem(col + s, columns)) for s in range(1, columns)]
+    meet(peers)
+
+    shards = (proj_ref, out_ref)
+    depth = proj_ref.shape[0]
+    width = proj_ref.shape[1]
+    half = depth // 2
+
+    def place(which, block_row, block_col, part=None):
+        first = 0 if part is None else part * half
+        size = depth if part is None else half
+        if which == 0:
+            return all_proj.at[
+                pl.ds(pl.multiple_of(block_row * depth + first, 16), size),
+                pl.ds(pl.multiple_of(block_col * width, width), width),
+            ]
+        return all_out.at[block_row, block_col, pl.ds(first, size)]
+
+    pending = []
+
+    def go(copy):
+        copy.start()
+        pending.append(copy)
+        return copy
+
+    part_copies = []
+    for s in range(1, columns):
+        target = lax.rem(col + s, columns)
+        part_copies.append(
+            go(
+                remote(
+                    maps_ref.at[target],
+                    parts.at[s - 1],
+                    part_send.at[s - 1],
+                    part_recv.at[s - 1],
+                    at_col(target),
+                )
+            )
+        )
+    line = {}
+
+    def start_line(which):
+        for s in range(1, rows):
+            line[which, s] = go(
+                remote(
+                    shards[which],
+                    place(which, row, col),
+                    line_send.at[which, s - 1],
+                    line_recv.at[which, s - 1],
+                    at_row(lax.rem(row + s, rows)),
+                )
+            )
+
+    start_line(0)
+    own = []
+    for which in range(2):
+        own.append(
+            pltpu.make_async_copy(shards[which], place(which, row, col), own_sem.at[which])
+        )
+        own[-1].start()
+
+    if square:
+        across = lax.rem(chip, 2)
+        upward = chip // 2
+        chip_x = upward * 2 + 1 - across
+        chip_y = (1 - upward) * 2 + across
+        chip_d = (1 - upward) * 2 + 1 - across
+        senders = [chip_x, chip_y]
+        targets = [chip_x, chip_y]
+    else:
+        targets = [lax.rem(chip + t, chips) for t in range(1, chips)]
+        senders = [lax.rem(chip + chips - t, chips) for t in range(1, chips)]
+
+    plane = {}
+    pair = {}
+
+    def to_pair(which, s, slot, source, target):
+        pair[which, s, slot] = go(
+            remote(
+                source,
+                target,
+                pair_send.at[which, s, slot],
+                pair_recv.at[which, s, slot],
+                at_col(sibling),
+            )
+        )
+
+    def spread(which, s):
+        block_row = lax.rem(row + rows - s, rows)
+        if s > 0:
+            line[which, s].wait_recv()
+            source = place(which, block_row, col)
+        else:
+            source = shards[which]
+        for t, target in enumerate(targets):
+            plane[which, s, t] = go(
+                remote(
+                    source,
+                    place(which, block_row, col),
+                    plane_send.at[which, s, t],
+                    plane_recv.at[which, s, t],
+                    at_col(target * 2 + core),
+                )
+            )
+        to_pair(which, s, 0, source, place(which, block_row, col))
+
+    def relay(which, s):
+        block_row = lax.rem(row + rows - s, rows)
+        for t, sender in enumerate(senders):
+            plane[which, s, t].wait_recv()
+            if square:
+                onward = place(which, block_row, sender * 2 + core, t)
+                plane[which, s, 2 + t] = go(
+                    remote(
+                        onward,
+                        onward,
+                        plane_send.at[which, s, 2 + t],
+                        plane_recv.at[which, s, 2 + t],
+                        at_col(targets[1 - t] * 2 + core),
+                    )
+                )
+            here = place(which, block_row, sender * 2 + core)
+            to_pair(which, s, 1 + t, here, here)
+
+    def corner(which, s):
+        if not square:
+            return
+        block_row = lax.rem(row + rows - s, rows)
+        for t in range(2):
+            plane[which, s, 2 + t].wait_recv()
+        here = place(which, block_row, chip_d * 2 + core)
+        to_pair(which, s, 3, here, here)
+
+    steps = [(which, s) for which in range(2) for s in range(rows)]
+    for i, step in enumerate(steps):
+        spread(*step)
+        if i == 0:
+            total = maps_ref[col].astype(jnp.float32)
+            for s in range(1, columns):
+                part_copies[s - 1].wait_recv()
+                total = total + parts[s - 1].astype(jnp.float32)
+            chunk[...] = total.astype(jnp.bfloat16)
+            map_copies = []
+            for s in range(1, columns):
+                map_copies.append(
+                    go(
+                        remote(
+                            chunk,
+                            all_maps.at[col],
+                            map_send.at[s - 1],
+                            map_recv.at[s - 1],
+                            at_col(lax.rem(col + s, columns)),
+                        )
+                    )
+                )
+            mine = pltpu.make_async_copy(chunk, all_maps.at[col], own_sem.at[2])
+            mine.start()
+            start_line(1)
+        if i >= 1:
+            relay(*steps[i - 1])
+        if i >= 2:
+            corner(*steps[i - 2])
+    relay(*steps[-1])
+    corner(*steps[-2])
+    corner(*steps[-1])
+    for key in pair:
+        pair[key].wait_recv()
+    for copy in map_copies:
+        copy.wait_recv()
+    for copy in own:
+        copy.wait()
+    mine.wait()
+    for copy in pending:
+        copy.wait_send()
+
+
+def gather_weights(projection_weight, output_weight, maps):
+    rows = lax.axis_size("row")
+    columns = lax.axis_size("col")
+    dma = pltpu.SemaphoreType.DMA
+    slots = 4 if columns == 8 else columns // 2
+    anywhere = pl.BlockSpec(memory_space=pl.ANY)
+    return pl.pallas_call(
+        functools.partial(gather_kernel, rows, columns),
+        out_shape=(
+            jax.ShapeDtypeStruct(
+                (projection_weight.shape[0] * rows, projection_weight.shape[1] * columns),
+                jnp.bfloat16,
+            ),
+            jax.ShapeDtypeStruct((rows, columns) + output_weight.shape, jnp.bfloat16),
+            jax.ShapeDtypeStruct(maps.shape, jnp.bfloat16),
+        ),
+        in_specs=[anywhere, anywhere, pl.BlockSpec(memory_space=pltpu.VMEM)],
+        out_specs=(anywhere, anywhere, anywhere),
+        scratch_shapes=[
+            pltpu.VMEM((columns - 1,) + maps.shape[1:], jnp.bfloat16),
+            pltpu.VMEM(maps.shape[1:], jnp.bfloat16),
+            dma((3,)),
+            dma((2, rows - 1)),
+            dma((2, rows - 1)),
+            dma((2, rows, slots)),
+            dma((2, rows, slots)),
+            dma((2, rows, slots)),
+            dma((2, rows, slots)),
+            dma((columns - 1,)),
+            dma((columns - 1,)),
+            dma((columns - 1,)),
+            dma((columns - 1,)),
+        ],
+        compiler_params=pltpu.CompilerParams(
+            collective_id=0, has_side_effects=True, vmem_limit_bytes=16 * 1024 * 1024
+        ),
+        name="gather_weights",
+    )(projection_weight, output_weight, maps)
+
+
+def share_kernel(columns, exchange, block_ref, all_ref, own_sem, send_sem, recv_sem):
+    row = lax.axis_index("row")
+    col = lax.axis_index("col")
+    others = [lax.rem(col + s, columns) for s in range(1, columns)]
+    meet([{"row": row, "col": other} for other in others])
+    copies = []
+    for s, other in enumerate(others):
+        copies.append(
+            remote(
+                block_ref.at[other] if exchange else block_ref,
+                all_ref.at[col],
+                send_sem.at[s],
+                recv_sem.at[s],
+                {"row": row, "col": other},
+            )
+        )
+        copies[-1].start()
+    mine = pltpu.make_async_copy(
+        block_ref.at[col] if exchange else block_ref, all_ref.at[col], own_sem
+    )
+    mine.start()
+    mine.wait()
+    for copy in copies:
+        copy.wait()
+
+
+def share(block, exchange, identity):
+    columns = lax.axis_size("col")
+    dma = pltpu.SemaphoreType.DMA
+    shape = block.shape if exchange else (columns,) + block.shape
+    return pl.pallas_call(
+        functools.partial(share_kernel, columns, exchange),
+        out_shape=jax.ShapeDtypeStruct(shape, block.dtype),
+        in_specs=[pl.BlockSpec(memory_space=pl.ANY)],
+        out_specs=pl.BlockSpec(memory_space=pl.ANY),
+        scratch_shapes=[dma, dma((columns - 1,)), dma((columns - 1,))],
+        compiler_params=pltpu.CompilerParams(
+            collective_id=identity, has_side_effects=True, vmem_limit_bytes=16 * 1024 * 1024
+        ),
+        name="exchange" if exchange else "share",
+    )(block)
 
 
 def local(
@@ -87,14 +408,6 @@
     adapter_row = lax.dynamic_index_in_dim(prompt_adapter, row_index, 0, keepdims=False)
     tok_index = col_index * token_rows + jnp.arange(token_rows, dtype=jnp.int32)
     prompt_of, within_prompt, token_positions = prompt_layout(lengths_row, tok_index)
-    wide_parts = (
-        lax.all_gather(projection_weight, "col", axis=1, tiled=True),
-        lax.all_gather(output_weight, "col", axis=1, tiled=True),
-    )
-    qkv_full, out_full = (
-        lax.all_gather(wide_parts[0], "row", axis=0, tiled=True),
-        lax.all_gather(wide_parts[1], "row", axis=0, tiled=True),
-    )
     owner_column = adapter_row // adapter_projection_down.shape[0]
     nearby_slot = adapter_row % adapter_projection_down.shape[0]
     owned_here = (owner_column == col_index)[:, None, None]
@@ -102,22 +415,37 @@
     def choose_experts(table):
         return jnp.where(owned_here, jnp.take(table, nearby_slot, axis=0).astype(jnp.float32), 0.0)
 
-    summed = (
-        lax.psum(choose_experts(adapter_projection_down).astype(jnp.bfloat16), "col").astype(
-            jnp.float32
-        ),
-        lax.psum(choose_experts(adapter_projection_up).astype(jnp.bfloat16), "col").astype(
-            jnp.float32
-        ),
-        lax.psum(choose_experts(adapter_output_down).astype(jnp.bfloat16), "col").astype(
-            jnp.float32
-        ),
-        lax.psum(choose_experts(adapter_output_up).astype(jnp.bfloat16), "col").astype(jnp.float32),
-    )
-    projection_down_map = summed[0].astype(jnp.bfloat16)
-    projection_up_map = summed[1].astype(jnp.bfloat16)
-    output_down_map = summed[2].astype(jnp.bfloat16)
-    output_up_map = summed[3].astype(jnp.bfloat16)
+    tables = (
+        adapter_projection_down,
+        adapter_projection_up,
+        adapter_output_down,
+        adapter_output_up,
+    )
+    chosen = jnp.concatenate(
+        [choose_experts(table).astype(jnp.bfloat16) for table in tables], axis=2
+    )
+    prompts, rank, map_width = chosen.shape
+    splits = columns // prompts
+    chosen = (
+        chosen.reshape(prompts, rank, splits, map_width // splits)
+        .transpose(0, 2, 1, 3)
+        .reshape(columns, rank, map_width // splits)
+    )
+    qkv_full, out_blocks, all_maps = gather_weights(projection_weight, output_weight, chosen)
+    out_full = out_blocks.transpose(0, 2, 1, 3).reshape(
+        output_weight.shape[0] * lax.axis_size("row"), output_weight.shape[1] * columns
+    )
+    all_maps = (
+        all_maps.reshape(prompts, splits, rank, map_width // splits)
+        .transpose(0, 2, 1, 3)
+        .reshape(prompts, rank, map_width)
+    )
+    cuts = []
+    for table in tables:
+        cuts.append((cuts[-1] if cuts else 0) + table.shape[2])
+    projection_down_map, projection_up_map, output_down_map, output_up_map = jnp.split(
+        all_maps, cuts[:-1], axis=2
+    )
     normalized = rms_scaled(hidden_input, attention_norm_gain)
     projection_all = jnp.dot(normalized, qkv_full, preferred_element_type=jnp.float32)
     projection_all = projection_all + adapter_scale * adapter_change(
@@ -142,10 +470,9 @@
     )
     query_index = jnp.tile(tok_index, QUERY_PER_KEY)
     query_prompt = jnp.tile(prompt_of, QUERY_PER_KEY)
-    segments = (
-        lax.all_gather(flattened_keys, "col", axis=0, tiled=True),
-        lax.all_gather(value_slice, "col", axis=0, tiled=True),
-    )
+    shared = share(jnp.concatenate([flattened_keys, value_slice], axis=1), False, 1)
+    shared = shared.reshape(columns * token_rows, 2 * KEY_HEADS * HEAD_SIZE)
+    segments = (shared[:, : KEY_HEADS * HEAD_SIZE], shared[:, KEY_HEADS * HEAD_SIZE :])
     best_experts = jnp.full((KEY_HEADS, QUERY_PER_KEY * token_rows), -1e30, jnp.float32)
     segment_length = segments[0].shape[0]
     key_lines = segments[0].reshape(segment_length, KEY_HEADS, HEAD_SIZE).transpose(1, 0, 2)
@@ -188,14 +515,15 @@
     local_experts = expert_gate_weight.shape[0]
     flat_routes = routes.reshape(-1)
     slots = route_slots(flat_routes, expert_total)
-    token_of = jnp.arange(flat_routes.shape[0], dtype=jnp.int32) // routes.shape[1]
-    dispatch_rows = (
-        jnp.zeros((expert_total, CAP, model_width), jnp.bfloat16)
-        .at[flat_routes, slots]
-        .set(normed_two[token_of])
-    )
-    sending = dispatch_rows.reshape(columns, local_experts, CAP, model_width)
-    arrived = lax.all_to_all(sending, "col", split_axis=0, concat_axis=0, tiled=True)
+    spots = (flat_routes * CAP + slots).reshape(routes.shape)
+    spot_index = jnp.arange(expert_total * CAP, dtype=jnp.int32)
+    marked = spots[:, :, None] == spot_index[None, None, :]
+    dispatch = jnp.any(marked, axis=1).astype(jnp.bfloat16)
+    sending = jnp.einsum(
+        "tj,td->jd", dispatch, normed_two, preferred_element_type=jnp.float32
+    ).astype(jnp.bfloat16)
+    sending = sending.reshape(columns, local_experts * CAP, model_width)
+    arrived = share(sending, True, 2).reshape(columns, local_experts, CAP, model_width)
     gate_vals = jnp.einsum(
         "sjcd,jdf->sjcf", arrived, expert_gate_weight, preferred_element_type=jnp.float32
     )
@@ -206,12 +534,14 @@
     answered = jnp.einsum(
         "sjcf,jfd->sjcd", hidden_vals, expert_down_weight, preferred_element_type=jnp.float32
     ).astype(jnp.bfloat16)
-    returned = lax.all_to_all(answered, "col", split_axis=0, concat_axis=0, tiled=True)
-    results = returned.reshape(expert_total, CAP, model_width)[flat_routes, slots]
-    combined = jnp.sum(
-        results.astype(jnp.float32).reshape(token_rows, routes.shape[1], model_width)
-        * mixing[:, :, None],
-        axis=1,
+    returned = share(
+        answered.reshape(columns, local_experts * CAP, model_width), True, 3
+    ).reshape(expert_total * CAP, model_width)
+    mix = jnp.sum(jnp.where(marked, mixing[:, :, None], 0.0), axis=1)
+    mix_high = mix.astype(jnp.bfloat16)
+    mix_low = (mix - mix_high.astype(jnp.float32)).astype(jnp.bfloat16)
+    combined = jnp.dot(mix_high, returned, preferred_element_type=jnp.float32) + jnp.dot(
+        mix_low, returned, preferred_element_type=jnp.float32
     )
     return (residual.astype(jnp.float32) + combined).astype(jnp.bfloat16)
 

time: 493 us -> 222 us (0.45)
  waiting for transfers between devices: 289 us -> 0 us
  Pallas kernels: 0 us -> 143 us
  local copies, waits for them, and re-layouts: 90.7 us -> 34.9 us
  blocking collectives: 48.8 us -> 0 us
  between operations: 13.7 us -> 0.54 us
    all_gather x4 -> x0, waiting for transfers between devices: 217 us -> none  [the longest x1 112 us: local(): lax.all_gather(wide_parts[0], 'row', axis=0, tiled=True)]
    pallas_call x0 -> x4, Pallas kernels: none -> 143 us  [the longest x1 79.5 us: gather_weights(): pl.pallas_call(functools.partial(gather_kernel, rows, columns), out_shape...]
    scatter x1 -> x0, local copies, waits for them, and re-layouts: 58.1 us -> none  [local(): dispatch_rows = jnp.zeros((expert_total, CAP, model_width), jnp.bfloat16)...]
    psum x1 -> x0, waiting for transfers between devices: 53 us -> none  [local(): lax.psum(choose_experts(adapter_output_up).astype(jnp.bfloat16), 'col')]
    all_to_all x1 -> x0, blocking collectives: 28.4 us -> none  [local(): lax.all_to_all(sending, 'col', split_axis=0, concat_axis=0, tiled=True)]
    all_gather x2 -> x0, blocking collectives: 20.4 us -> none  [the longest x1 10.6 us: local(): lax.all_gather(flattened_keys, 'col', axis=0, tiled=True)]
    all_to_all x1 -> x0, waiting for transfers between devices: 17 us -> none  [local(): lax.all_to_all(answered, 'col', split_axis=0, concat_axis=0, tiled=True)]
    gather x2 -> x0, local copies, waits for them, and re-layouts: 12.7 us -> none  [the longest x1 9.69 us: local(): returned.reshape(expert_total, CAP, model_width)[flat_routes, slots]]
  transfers between devices with their start and end apart: 6 -> 0, of which waited for: 6 -> 0; matrix products, arithmetic and copies ran while one was open for 7% -> 0% of each run, Pallas kernels for 0% -> 0%
where the time goes in v1:
time: 222 us; the launch traced here: 221 us
  Pallas kernels  143 us (64%)
  local copies, waits for them, and re-layouts  34.9 us (16%)
  matrix products  28.9 us (13%)
  other arithmetic  14.1 us (6%)
    pallas_call x1, Pallas kernels, gather_weights(): pl.pallas_call(functools.partial(gather_kernel, rows, columns), out_shape...  79.5 us
    pallas_call x3, Pallas kernels, share(): pl.pallas_call(functools.partial(share_kernel, columns, exchange), out_sh...  63 us
    transpose x1, local copies, waits for them, and re-layouts, local(): out_blocks.transpose(0, 2, 1, 3)  10.2 us
    dot_general x1, matrix products, local(): jnp.einsum('sjcf,jfd->sjcd', hidden_vals, expert_down_weight, preferred_e...  8.83 us
    unnamed x42, local copies, waits for them, and re-layouts  8.47 us
    dot_general x1, matrix products, local(): jnp.einsum('sjcd,jdf->sjcf', arrived, expert_up_weight, preferred_element...  5.34 us
    gather x4, local copies, waits for them, and re-layouts, choose_experts(): jnp.take(table, nearby_slot, axis=0).astype(jnp.float32)  5.06 us

profile of v1, /device:TPU:1, one launch (start us, length us, event | category | flops | bytes accessed | tf_op | source)
XLA Modules:
  0.0 220.9 jit_solution(3904382703718571778)
XLA Ops:
  3.2 1.2 fusion.51
  8.1 1.2 reduce-window.11
  12.8 1.5 gather_fusion.4
  14.4 1.5 gather_fusion.3
  15.9 1.5 gather_fusion.2
  18.5 1.7 fusion.13
  20.2 79.5 %gather_weights.1 = (bf16[1536,2048]{1,0:T(8,128)(2,1)S(1)}, bf16[4,8,384,192]{3,2,1,0:T(8,128)(2,1)S(1)}, bf16[8,16,3328]{2,1,0:T(8,128)(2,1)S(1)}) custom-call(bf16[384,256]{1,0:T(8,128)(2,1)S(1)} %copy-done.3, bf16[384,192]{1,0:T(8,128)(2,1)S(1)} %copy.77.out_ref, bf16[8,16,3328]{2,1,0:T(8,128)(2,1)S(1)} %bitcast.157), custom_call_target="tpu_custom_call" | custom-call | tf_op jit(solution)/shard_map/gather_weights/pallas_call | solution.py:307
  100.9 1.6 copy-done.2
  103.4 1.9 fusion.22
  106.8 13.9 %share.1 = bf16[8,128,512]{2,1,0:T(8,128)(2,1)S(1)} custom-call(bf16[128,512]{1,0:T(8,128)(2,1)S(1)} %pad_maximum_fusion.3.block_ref), custom_call_target="tpu_custom_call" | custom-call | tf_op jit(solution)/shard_map/share/pallas_call | solution.py:371
  121.8 10.2 %copy.88 = bf16[4,384,8,192]{1,0,3,2:T(4,128)(2,1)} copy(bf16[4,384,8,192]{3,1,2,0:T(8,128)(2,1)} %bitcast.155) | data formatting | bytes 9437184 | tf_op jit(solution)/shard_map/transpose | solution.py:435
  132.0 5.4 %copy.109 = bf16[192,8,4,384]{3,1,2,0:T(8,128)(2,1)} copy(bf16[192,8,4,384]{3,2,1,0:T(4,128)(2,1)} %bitcast.162) | data formatting | bytes 9437184
  137.4 1.5 select_reduce_fusion
  138.9 2.2 fusion
  141.1 1.8 fusion.43
  143.2 1.5 fusion.20
  144.7 4.1 %multiply_reduce_fusion = (f32[128]{0:T(128)S(1)}, f32[128,1536]{1,0:T(8,128)S(1)}) fusion(f32[128,1536]{1,0:T(8,128)S(1)} %fusion.20, bf16[128,1536]{0,1:T(8,128)(2,1)S(1)} %bitcast.164, bf16[1536,1536]{0,1:T(8,128)(2,1)} %bitcast.161, bf16[128,1536]{1,0:T(8,128)(2,1)S(1)} %copy-done.4), kind=kOutput, calls=%fused_computation.57 | convolution fusion | flops 605355904 | bytes 7078400 | tf_op jit(solution)/shard_map/dot_general | solution.py:505
  149.1 3.8 %gather_fusion.1 = f32[512]{0:T(512)S(1)} fusion(f32[128,16]{0,1:T(8,128)S(1)} %fusion.90, s32[512]{0:T(512)S(1)} %reshape.428), kind=kCustom, calls=%fused_computation.4 | custom fusion | bytes 8192 | tf_op jit(solution)/shard_map/jit(take_along_axis)/gather | solution.py:512
  154.1 24.6 %exchange.2 = bf16[8,80,1536]{2,1,0:T(8,128)(2,1)S(1)} custom-call(bf16[8,80,1536]{2,1,0:T(8,128)(2,1)S(1)} %bitcast.153), custom_call_target="tpu_custom_call" | custom-call | tf_op jit(solution)/shard_map/exchange/pallas_call | solution.py:371
  178.8 5.3 %fusion.4 = f32[2,8,40,768]{3,2,1,0:T(8,128)} fusion(bf16[2,1536,768]{2,1,0:T(8,128)(2,1)} %param.32, bf16[8,2,40,1536]{3,2,1,0:T(8,128)(2,1)S(1)} %bitcast.158), kind=kOutput, calls=%fused_computation.11 | convolution fusion | flops 1509949440 | bytes 8650752 | tf_op jit(solution)/shard_map/sjcd,jdf->sjcf/dot_general | solution.py:530
  184.1 8.8 %fusion.15 = bf16[8,2,40,1536]{3,2,0,1:T(8,128)(2,1)} fusion(bf16[2,768,1536]{2,1,0:T(8,128)(2,1)} %param.33, f32[2,8,40,768]{3,2,1,0:T(8,128)} %fusion.4, bf16[2,1536,768]{2,1,0:T(8,128)(2,1)} %param.31, bf16[8,2,40,1536]{3,2,1,0:T(8,128)(2,1)S(1)} %bitcast.159), kind=kOutput, calls=%fused_computation.21 | convolution fusion | flops 3022356480 | bytes 15335424 | tf_op jit(solution)/shard_map/sjcf,jfd->sjcd/dot_general | solution.py:534
  193.0 1.7 copy.98
  194.7 24.5 %exchange.3 = bf16[8,80,1536]{2,1,0:T(8,128)(2,1)S(1)} custom-call(bf16[8,80,1536]{2,1,0:T(8,128)(2,1)S(1)} %bitcast.154), custom_call_target="tpu_custom_call" | custom-call | tf_op jit(solution)/shard_map/exchange/pallas_call | solution.py:371
  219.7 1.2 fusion.23
  (107 shorter events, 18.2 us)
Async XLA Ops:
  0.0 17.8 %copy-start = (bf16[4,16,2048]{2,1,0:T(8,128)(2,1)S(1)}, bf16[4,16,2048]{2,1,0:T(8,128)(2,1)}, u32[]{:S(2)}) copy-start(bf16[4,16,2048]{2,1,0:T(8,128)(2,1)} %param.28) | copy-start | bytes 786436
  0.0 17.6 %copy-start.13 = (bf16[384,192]{0,1:T(8,128)(2,1)S(1)}, bf16[384,192]{0,1:T(8,128)(2,1)}, u32[]{:S(2)}) copy-start(bf16[384,192]{0,1:T(8,128)(2,1)} %param.25) | copy-start | bytes 442372
  1.1 102.3 %copy-start.16 = (pred[128,4]{0,1:T(4,128)(4,1)}, pred[128,4]{0,1:T(4,128)(4,1)S(1)}, u32[]{:S(2)}) copy-start(pred[128,4]{0,1:T(4,128)(4,1)S(1)} %iota_compare_fusion.5) | copy-start | bytes 1540
  7.0 8.8 %copy-start.7 = (f32[128,64]{0,1:T(8,128)}, f32[128,64]{0,1:T(8,128)S(1)}, u32[]{:S(2)}) copy-start(f32[128,64]{0,1:T(8,128)S(1)} %get-tuple-element.22) | copy-start | bytes 98308
  7.1 8.8 %copy-start.9 = (f32[128,64]{0,1:T(8,128)}, f32[128,64]{0,1:T(8,128)S(1)}, u32[]{:S(2)}) copy-start(f32[128,64]{0,1:T(8,128)S(1)} %get-tuple-element.23) | copy-start | bytes 98308
  12.8 7.4 %copy-start.3 = (bf16[384,256]{1,0:T(8,128)(2,1)S(1)}, bf16[384,256]{1,0:T(8,128)(2,1)}, u32[]{:S(2)}) copy-start(bf16[384,256]{1,0:T(8,128)(2,1)} %proj_ref.1) | copy-start | bytes 589828
  17.4 82.4 %copy-start.4 = (bf16[128,1536]{1,0:T(8,128)(2,1)S(1)}, bf16[128,1536]{1,0:T(8,128)(2,1)}, u32[]{:S(2)}) copy-start(bf16[128,1536]{1,0:T(8,128)(2,1)} %param.18) | copy-start | bytes 1179652
  99.8 2.7 %copy-start.2 = (bf16[4,8,384,192]{3,2,1,0:T(8,128)(2,1)}, bf16[4,8,384,192]{3,2,1,0:T(8,128)(2,1)S(1)}, u32[]{:S(2)}) copy-start(bf16[4,8,384,192]{3,2,1,0:T(8,128)(2,1)S(1)} %get-tuple-element.11) | copy-start | bytes 14155780
  103.4 2.3 %copy-start.8 = (f32[128,64]{0,1:T(8,128)S(1)}, f32[128,64]{0,1:T(8,128)}, u32[]{:S(2)}) copy-start(f32[128,64]{0,1:T(8,128)} %copy-done.7) | copy-start | bytes 98308
  103.4 2.3 %copy-start.10 = (f32[128,64]{0,1:T(8,128)S(1)}, f32[128,64]{0,1:T(8,128)}, u32[]{:S(2)}) copy-start(f32[128,64]{0,1:T(8,128)} %copy-done.9) | copy-start | bytes 98308
  105.3 0.9 copy-start.11
  105.4 0.8 copy-start.12
  132.0 5.4 %copy-start.5 = (pred[768,1024]{1,0:T(8,128)(4,1)S(1)}, pred[768,1024]{1,0:T(8,128)(4,1)}, u32[]{:S(2)}) copy-start(pred[768,1024]{1,0:T(8,128)(4,1)} %fusion.13) | copy-start | bytes 2359300
  141.1 2.1 copy-start.17
  144.7 4.1 %copy-start.15 = (bf16[1536,16]{0,1:T(8,128)(2,1)S(1)}, bf16[1536,16]{0,1:T(8,128)(2,1)}, u32[]{:S(2)}) copy-start(bf16[1536,16]{0,1:T(8,128)(2,1)} %param.26) | copy-start | bytes 147460
  149.1 3.9 %copy-start.14 = (s32[128,4]{0,1:T(4,128)S(1)}, s32[128,4]{0,1:T(4,128)}, u32[]{:S(2)}) copy-start(s32[128,4]{0,1:T(4,128)} %param.21) | copy-start | bytes 6148
  149.1 4.2 %copy-start.6 = (pred[128,640]{1,0:T(8,128)(4,1)S(1)}, pred[128,640]{1,0:T(8,128)(4,1)}, u32[]{:S(2)}) copy-start(pred[128,640]{1,0:T(8,128)(4,1)} %fusion.37) | copy-start | bytes 245764
  219.2 1.7 copy-start.1

commit v2 on v1

--- a/solution.py
+++ b/solution.py
@@ -128,17 +128,21 @@
     shards = (proj_ref, out_ref)
     depth = proj_ref.shape[0]
     width = proj_ref.shape[1]
-    half = depth // 2
+    out_depth, out_width = out_ref.shape
 
     def place(which, block_row, block_col, part=None):
-        first = 0 if part is None else part * half
-        size = depth if part is None else half
+        tall = depth if which == 0 else out_depth
+        first = 0 if part is None else part * (tall // 2)
+        size = tall if part is None else tall // 2
         if which == 0:
             return all_proj.at[
                 pl.ds(pl.multiple_of(block_row * depth + first, 16), size),
                 pl.ds(pl.multiple_of(block_col * width, width), width),
             ]
-        return all_out.at[block_row, block_col, pl.ds(first, size)]
+        return all_out.at[
+            pl.ds(pl.multiple_of(block_row * out_depth + first, 16), size),
+            pl.ds(pl.multiple_of(block_col * out_width, 128), out_width),
+        ]
 
     pending = []
 
@@ -311,7 +315,9 @@
                 (projection_weight.shape[0] * rows, projection_weight.shape[1] * columns),
                 jnp.bfloat16,
             ),
-            jax.ShapeDtypeStruct((rows, columns) + output_weight.shape, jnp.bfloat16),
+            jax.ShapeDtypeStruct(
+                (output_weight.shape[0] * rows, output_weight.shape[1] * columns), jnp.bfloat16
+            ),
             jax.ShapeDtypeStruct(maps.shape, jnp.bfloat16),
         ),
         in_specs=[anywhere, anywhere, pl.BlockSpec(memory_space=pltpu.VMEM)],
@@ -379,6 +385,174 @@
         ),
         name="exchange" if exchange else "share",
     )(block)
+
+
+def experts_kernel(
+    columns,
+    sending_ref,
+    gate_ref,
+    up_ref,
+    down_ref,
+    all_ref,
+    gate,
+    up,
+    down,
+    arrived,
+    answer,
+    load_sem,
+    own_sem,
+    send_sem,
+    recv_sem,
+    back_send,
+    back_recv,
+):
+    row = lax.axis_index("row")
+    col = lax.axis_index("col")
+    chips = columns // 2
+    core = lax.rem(col, 2)
+    chip = col // 2
+    meet([{"row": row, "col": lax.rem(col + s, columns)} for s in range(1, columns)])
+    loads = [
+        pltpu.make_async_copy(gate_ref, gate, load_sem.at[0]),
+        pltpu.make_async_copy(up_ref, up, load_sem.at[1]),
+        pltpu.make_async_copy(down_ref, down, load_sem.at[2]),
+    ]
+    for load in loads:
+        load.start()
+    if chips == 4:
+        across = lax.rem(chip, 2)
+        upward = chip // 2
+        targets = [
+            chip,
+            upward * 2 + 1 - across,
+            (1 - upward) * 2 + across,
+            (1 - upward) * 2 + 1 - across,
+        ]
+        sources = targets
+    else:
+        targets = [lax.rem(chip + t, chips) for t in range(chips)]
+        sources = [lax.rem(chip + chips - t, chips) for t in range(chips)]
+    rows = sending_ref.shape[1]
+    cap = rows // gate_ref.shape[0]
+
+    def outward(g, other):
+        target = targets[g] * 2 + other
+        return remote(
+            sending_ref.at[target],
+            arrived.at[2 * g + core],
+            send_sem.at[2 * g + other],
+            recv_sem.at[2 * g + core],
+            {"row": row, "col": target},
+        )
+
+    def inward(g, other):
+        return remote(
+            sending_ref.at[col],
+            arrived.at[2 * g + other],
+            send_sem.at[2 * g + other],
+            recv_sem.at[2 * g + other],
+            {"row": row, "col": targets[g] * 2 + other},
+        )
+
+    def back(g, other):
+        return remote(
+            answer.at[2 * g + other],
+            all_ref.at[col],
+            back_send.at[2 * g + other],
+            back_recv.at[2 * g + core],
+            {"row": row, "col": sources[g] * 2 + other},
+        )
+
+    def back_in(g, other):
+        return remote(
+            answer.at[2 * g + other],
+            all_ref.at[targets[g] * 2 + other],
+            back_send.at[2 * g + other],
+            back_recv.at[2 * g + other],
+            {"row": row, "col": targets[g] * 2 + other},
+        )
+
+    def members(g):
+        return [1 - core] if g == 0 else [0, 1]
+
+    def work(g):
+        held = jnp.concatenate([arrived[2 * g], arrived[2 * g + 1]], axis=0)
+        spot = lax.broadcasted_iota(jnp.int32, (2 * rows, 1), 0)
+        spot = jnp.where(spot >= rows, spot - rows, spot)
+        total = None
+        for j in range(gate.shape[0]):
+            gate_vals = jnp.dot(held, gate[j], preferred_element_type=jnp.float32)
+            up_vals = jnp.dot(held, up[j], preferred_element_type=jnp.float32)
+            mine = (spot >= j * cap) & (spot < (j + 1) * cap)
+            hidden = jnp.where(mine, jnp.maximum(gate_vals, 0.0) * up_vals, 0.0)
+            part = jnp.dot(
+                hidden.astype(jnp.bfloat16), down[j], preferred_element_type=jnp.float32
+            )
+            total = part if total is None else total + part
+        total = total.astype(jnp.bfloat16)
+        answer[2 * g] = total[:rows]
+        answer[2 * g + 1] = total[rows:]
+
+    first = min(chips, 3)
+    sent = []
+    for g in list(range(1, first)) + [0]:
+        for other in members(g):
+            sent.append(outward(g, other))
+            sent[-1].start()
+    mine = pltpu.make_async_copy(sending_ref.at[col], arrived.at[core], own_sem.at[0])
+    mine.start()
+    for load in loads:
+        load.wait()
+    mine.wait()
+    for g in range(chips):
+        for other in members(g):
+            inward(g, other).wait_recv()
+        work(g)
+        if g == 0:
+            for late in range(first, chips):
+                for other in members(late):
+                    sent.append(outward(late, other))
+                    sent[-1].start()
+            kept = pltpu.make_async_copy(answer.at[core], all_ref.at[col], own_sem.at[1])
+            kept.start()
+        for other in members(g):
+            sent.append(back(g, other))
+            sent[-1].start()
+    for g in range(chips):
+        for other in members(g):
+            back_in(g, other).wait_recv()
+    kept.wait()
+    for copy in sent:
+        copy.wait_send()
+
+
+def run_experts(sending, gate, up, down):
+    columns = lax.axis_size("col")
+    dma = pltpu.SemaphoreType.DMA
+    anywhere = pl.BlockSpec(memory_space=pl.ANY)
+    return pl.pallas_call(
+        functools.partial(experts_kernel, columns),
+        out_shape=jax.ShapeDtypeStruct(sending.shape, jnp.bfloat16),
+        in_specs=[pl.BlockSpec(memory_space=pltpu.VMEM), anywhere, anywhere, anywhere],
+        out_specs=anywhere,
+        scratch_shapes=[
+            pltpu.VMEM(gate.shape, jnp.bfloat16),
+            pltpu.VMEM(up.shape, jnp.bfloat16),
+            pltpu.VMEM(down.shape, jnp.bfloat16),
+            pltpu.VMEM(sending.shape, jnp.bfloat16),
+            pltpu.VMEM(sending.shape, jnp.bfloat16),
+            dma((3,)),
+            dma((2,)),
+            dma((columns,)),
+            dma((columns,)),
+            dma((columns,)),
+            dma((columns,)),
+        ],
+        compiler_params=pltpu.CompilerParams(
+            collective_id=2, has_side_effects=True, vmem_limit_bytes=40 * 1024 * 1024
+        ),
+        name="run_experts",
+    )(sending, gate, up, down)
 
 
 def local(
@@ -408,12 +582,17 @@
     adapter_row = lax.dynamic_index_in_dim(prompt_adapter, row_index, 0, keepdims=False)
     tok_index = col_index * token_rows + jnp.arange(token_rows, dtype=jnp.int32)
     prompt_of, within_prompt, token_positions = prompt_layout(lengths_row, tok_index)
-    owner_column = adapter_row // adapter_projection_down.shape[0]
-    nearby_slot = adapter_row % adapter_projection_down.shape[0]
-    owned_here = (owner_column == col_index)[:, None, None]
+    adapter_count = adapter_projection_down.shape[0]
 
     def choose_experts(table):
-        return jnp.where(owned_here, jnp.take(table, nearby_slot, axis=0).astype(jnp.float32), 0.0)
+        return sum(
+            jnp.where(
+                (adapter_row == col_index * adapter_count + a)[:, None, None],
+                table[a][None].astype(jnp.float32),
+                0.0,
+            )
+            for a in range(adapter_count)
+        )
 
     tables = (
         adapter_projection_down,
@@ -431,10 +610,20 @@
         .transpose(0, 2, 1, 3)
         .reshape(columns, rank, map_width // splits)
     )
-    qkv_full, out_blocks, all_maps = gather_weights(projection_weight, output_weight, chosen)
-    out_full = out_blocks.transpose(0, 2, 1, 3).reshape(
-        output_weight.shape[0] * lax.axis_size("row"), output_weight.shape[1] * columns
-    )
+    out_depth, out_width = output_weight.shape
+    paired = out_width == 192
+    if paired:
+        side = output_weight[:, 128:]
+        packed = jnp.concatenate(
+            [
+                output_weight[:, :128],
+                jnp.concatenate([side[: out_depth // 2], side[out_depth // 2 :]], axis=1),
+            ],
+            axis=0,
+        )
+    else:
+        packed = jnp.pad(output_weight, ((0, 0), (0, -out_width % 128)))
+    qkv_full, out_packed, all_maps = gather_weights(projection_weight, packed, chosen)
     all_maps = (
         all_maps.reshape(prompts, splits, rank, map_width // splits)
         .transpose(0, 2, 1, 3)
@@ -502,14 +691,47 @@
         .reshape(token_rows, QUERY_HEADS * HEAD_SIZE)
         .astype(jnp.bfloat16)
     )
-    projected_rows = jnp.dot(attention_result, out_full, preferred_element_type=jnp.float32)
+    row_count = lax.axis_size("row")
+    if paired:
+        stacked = out_packed.reshape(row_count, packed.shape[0], columns * 128)
+        attended_parts = attention_result.reshape(token_rows, row_count, out_depth)
+        front = jnp.einsum(
+            "trk,rkn->tn",
+            attended_parts,
+            stacked[:, :out_depth],
+            preferred_element_type=jnp.float32,
+        ).reshape(token_rows, columns, 128)
+        halves = [
+            jnp.einsum(
+                "trk,rkn->tn",
+                attended_parts[:, :, h * (out_depth // 2) : (h + 1) * (out_depth // 2)],
+                stacked[:, out_depth:],
+                preferred_element_type=jnp.float32,
+            ).reshape(token_rows, columns, 128)[:, :, h * 64 : (h + 1) * 64]
+            for h in range(2)
+        ]
+        projected_rows = jnp.concatenate([front, halves[0] + halves[1]], axis=2)
+    else:
+        projected_rows = jnp.dot(
+            attention_result, out_packed, preferred_element_type=jnp.float32
+        ).reshape(token_rows, columns, packed.shape[1])[:, :, :out_width]
+    projected_rows = projected_rows.reshape(token_rows, model_width)
     projected_rows = projected_rows + adapter_scale * adapter_change(
         attention_result, within_prompt, output_down_map, output_up_map
     )
     residual = (hidden_input.astype(jnp.float32) + projected_rows).astype(jnp.bfloat16)
     normed_two = rms_scaled(residual, expert_norm_gain)
     logits = jnp.dot(normed_two, router, preferred_element_type=jnp.float32)
-    squashed = jax.nn.sigmoid(jnp.take_along_axis(logits, routes, axis=1))
+    squashed = jax.nn.sigmoid(
+        jnp.sum(
+            jnp.where(
+                routes[:, :, None] == jnp.arange(router.shape[1], dtype=jnp.int32)[None, None, :],
+                logits[:, None, :],
+                0.0,
+            ),
+            axis=2,
+        )
+    )
     mixing = squashed / jnp.sum(squashed, axis=1, keepdims=True)
     expert_total = router.shape[1]
     local_experts = expert_gate_weight.shape[0]
@@ -523,19 +745,8 @@
         "tj,td->jd", dispatch, normed_two, preferred_element_type=jnp.float32
     ).astype(jnp.bfloat16)
     sending = sending.reshape(columns, local_experts * CAP, model_width)
-    arrived = share(sending, True, 2).reshape(columns, local_experts, CAP, model_width)
-    gate_vals = jnp.einsum(
-        "sjcd,jdf->sjcf", arrived, expert_gate_weight, preferred_element_type=jnp.float32
-    )
-    up_vals = jnp.einsum(
-        "sjcd,jdf->sjcf", arrived, expert_up_weight, preferred_element_type=jnp.float32
-    )
-    hidden_vals = (jnp.maximum(gate_vals, 0.0) * up_vals).astype(jnp.bfloat16)
-    answered = jnp.einsum(
-        "sjcf,jfd->sjcd", hidden_vals, expert_down_weight, preferred_element_type=jnp.float32
-    ).astype(jnp.bfloat16)
-    returned = share(
-        answered.reshape(columns, local_experts * CAP, model_width), True, 3
+    returned = run_experts(
+        sending, expert_gate_weight, expert_up_weight, expert_down_weight
     ).reshape(expert_total * CAP, model_width)
     mix = jnp.sum(jnp.where(marked, mixing[:, :, None], 0.0), axis=1)
     mix_high = mix.astype(jnp.bfloat16)

time: 222 us -> 193 us (0.87)
  local copies, waits for them, and re-layouts: 34.9 us -> 22.5 us
  Pallas kernels: 143 us -> 134 us
  matrix products: 28.9 us -> 22.2 us
    pallas_call x3 -> x1, Pallas kernels: 63 us -> 13.9 us  [share(): pl.pallas_call(functools.partial(share_kernel, columns, exchange), out_sh...]
    pallas_call x0 -> x1, Pallas kernels: none -> 46.5 us  [run_experts(): pl.pallas_call(functools.partial(experts_kernel, columns), out_shape=jax....]
    dot_general x3, matrix products: 18.3 us -> 7.47 us  [the longest x2 4.42 us: local(): jnp.einsum('trk,rkn->tn', attended_parts[:, :, h * (out_depth // 2):(h +...]
    transpose x1 -> x0, local copies, waits for them, and re-layouts: 10.2 us -> none  [local(): out_blocks.transpose(0, 2, 1, 3)]
    gather x9 -> x0, local copies, waits for them, and re-layouts: 9.2 us -> none  [the longest x4 5.06 us: choose_experts(): jnp.take(table, nearby_slot, axis=0).astype(jnp.float32)]
    pallas_call x1, Pallas kernels: 79.5 us -> 73.6 us  [gather_weights(): pl.pallas_call(functools.partial(gather_kernel, rows, columns), out_shape...]
    dot_general x0 -> x2, local copies, waits for them, and re-layouts: none -> 5.01 us  [local(): jnp.einsum('trk,rkn->tn', attended_parts, stacked[:, :out_depth], preferr...]
    dot_general x1, matrix products: 1.08 us -> 3.82 us  [local(): jnp.dot(normalized, qkv_full, preferred_element_type=jnp.float32)]
where the time goes in v2:
time: 193 us; the launch traced here: 192 us
  Pallas kernels  134 us (69%)
  local copies, waits for them, and re-layouts  22.5 us (12%)
  matrix products  22.2 us (12%)
  other arithmetic  12.6 us (7%)
    pallas_call x1, Pallas kernels, gather_weights(): pl.pallas_call(functools.partial(gather_kernel, rows, columns), out_shape...  73.6 us
    pallas_call x1, Pallas kernels, run_experts(): pl.pallas_call(functools.partial(experts_kernel, columns), out_shape=jax....  46.5 us
    pallas_call x1, Pallas kernels, share(): pl.pallas_call(functools.partial(share_kernel, columns, exchange), out_sh...  13.9 us
    unnamed x43, local copies, waits for them, and re-layouts  11 us
    dot_general x2, local copies, waits for them, and re-layouts, local(): jnp.einsum('trk,rkn->tn', attended_parts, stacked[:, :out_depth], preferr...  5.01 us
    dot_general x2, matrix products, local(): jnp.einsum('trk,rkn->tn', attended_parts[:, :, h * (out_depth // 2):(h +...  4.42 us
    reduce_sum x1, other arithmetic, local(): running_new = jnp.sum(weights, axis=-1)  4.12 us
    dot_general x1, matrix products, local(): jnp.einsum('hqd,hkd->hqk', grouped, key_lines, preferred_element_type=jnp...  4.09 us

profile of v2, /device:TPU:1, one launch (start us, length us, event | category | flops | bytes accessed | tf_op | source)
XLA Modules:
  0.0 191.9 jit_solution(12789841942217837613)
XLA Ops:
  1.1 0.9 slice.121
  4.0 1.0 bitcast_convert_fusion.7
  5.7 73.6 %gather_weights.1 = (bf16[1536,2048]{1,0:T(8,128)(2,1)S(1)}, bf16[2304,1024]{1,0:T(8,128)(2,1)S(1)}, bf16[8,16,3328]{2,1,0:T(8,128)(2,1)S(1)}) custom-call(bf16[384,256]{1,0:T(8,128)(2,1)S(1)} %copy-done.5, bf16[576,128]{1,0:T(8,128)(2,1)S(1)} %maximum_maximum_fusion.out_ref, bf16[8,16,3328]{2,1,0:T(8,128)(2,1)S(1)} %bitcast.181), custom_call_target="tpu_custom_call" | custom-call | tf_op jit(solution)/shard_map/gather_weights/pallas_call | solution.py:311
  79.4 2.7 %copy-done.1 = bf16[1536,2048]{1,0:T(8,128)(2,1)} copy-done((bf16[1536,2048]{1,0:T(8,128)(2,1)}, bf16[1536,2048]{1,0:T(8,128)(2,1)S(1)}, u32[]{:S(2)}) %copy-start.1) | copy-done | bytes 6291480
  82.1 2.2 %copy-done.4 = bf16[2304,1024]{1,0:T(8,128)(2,1)} copy-done((bf16[2304,1024]{1,0:T(8,128)(2,1)}, bf16[2304,1024]{1,0:T(8,128)(2,1)S(1)}, u32[]{:S(2)}) %copy-start.4) | copy-done | bytes 4718616
  84.6 1.7 fusion.4
  86.5 3.8 %fusion.47 = f32[128,2048]{1,0:T(8,128)S(1)} fusion(bf16[1536,2048]{1,0:T(8,128)(2,1)} %copy-done.1, bf16[128,1536]{1,0:T(8,128)(2,1)S(1)} %copy-done.6, f32[1536]{0:T(1024)S(1)} %convert_element_type.126, f32[128]{0:T(128)S(1)} %add_rsqrt_fusion.1), kind=kOutput, calls=%fused_computation.72 | convolution fusion | flops 806092800 | bytes 7739904 | tf_op jit(solution)/shard_map/dot_general | solution.py:639
  91.3 0.9 slice.159
  92.2 1.4 copy.109
  95.2 13.9 %share.1 = bf16[8,128,512]{2,1,0:T(8,128)(2,1)S(1)} custom-call(bf16[128,512]{1,0:T(8,128)(2,1)S(1)} %pad_maximum_fusion.4.block_ref), custom_call_target="tpu_custom_call" | custom-call | tf_op jit(solution)/shard_map/share/pallas_call | solution.py:377
  109.7 4.1 %select_reduce_fusion = (f32[2,768]{1,0:T(2,128)S(1)}, f32[2,768,1024]{2,1,0:T(8,128)}) fusion(pred[768,1024]{1,0:T(8,128)(4,1)S(1)} %copy-done.12, bf16[2,768,128]{2,1,0:T(8,128)(2,1)S(1)} %bitcast.199, bf16[1024,2,128]{2,0,1:T(8,128)(2,1)S(1)} %copy.114), kind=kOutput, calls=%fused_computation.1 | convolution fusion | flops 407370240 | bytes 8001536 | tf_op jit(solution)/shard_map/hqd,hkd->hqk/dot_general | solution.py:674
  114.3 4.1 %fusion = f32[2,768]{1,0:T(2,128)S(1)} fusion(f32[2,768,1024]{2,1,0:T(8,128)} %get-tuple-element.46, f32[2,768]{1,0:T(2,128)S(1)} %broadcast_maximum_fusion, pred[768,1024]{1,0:T(8,128)(4,1)S(1)} %copy-done.12), kind=kLoop, calls=%fused_computation.2 | loop fusion | flops 6289920 | bytes 7090176 | tf_op jit(solution)/shard_map/reduce_sum | solution.py:680
  118.9 1.6 fusion.25
  120.8 2.3 %fusion.15 = f32[128,1024,1]{0,1,2:T(8,128)S(1)} fusion(bf16[4,576,1024]{2,1,0:T(8,128)(2,1)} %bitcast.182, bf16[128,4,384]{0,2,1:T(8,128)(2,1)S(1)} %bitcast.187), kind=kOutput, calls=%fused_computation.22 | convolution fusion | flops 201326592 | bytes 2293760 | tf_op jit(solution)/shard_map/trk,rkn->tn/dot_general | solution.py:705
  123.0 2.1 %fusion.17 = f32[128,1024,1]{0,1,2:T(8,128)S(1)} fusion(bf16[4,576,1024]{2,1,0:T(8,128)(2,1)} %bitcast.183, bf16[128,4,384]{0,2,1:T(8,128)(2,1)S(1)} %bitcast.188), kind=kOutput, calls=%fused_computation.24 | convolution fusion | flops 201326592 | bytes 2293760 | tf_op jit(solution)/shard_map/trk,rkn->tn/dot_general | solution.py:705
  125.2 2.2 %slice_bitcast_fusion = bf16[1024,384,4]{0,1,2:T(8,128)(2,1)S(1)} fusion(bf16[4,576,1024]{2,1,0:T(8,128)(2,1)} %bitcast.184), kind=kLoop, calls=%fused_computation.5 | loop fusion | bytes 6291456 | tf_op jit(solution)/shard_map/trk,rkn->tn/dot_general | solution.py:698
  127.4 2.8 %copy.118 = bf16[1024,384,4]{1,0,2:T(8,128)(2,1)} copy(bf16[1024,384,4]{0,1,2:T(8,128)(2,1)S(1)} %slice_bitcast_fusion) | data formatting | bytes 6291456 | tf_op jit(solution)/shard_map/trk,rkn->tn/dot_general | solution.py:698
  130.3 3.1 %convolution_bitcast_fusion.2 = f32[128,8,128]{0,2,1:T(8,128)S(1)} fusion(bf16[128,4,384,1]{0,2,3,1:T(8,128)(2,1)} %bitcast.189, bf16[8,128,384,4]{2,1,0,3:T(8,128)(2,1)} %bitcast.186), kind=kOutput, calls=%fused_computation.29 | convolution fusion | flops 402653184 | bytes 4063232 | tf_op jit(solution)/shard_map/trk,rkn->tn/dot_general | solution.py:698
  133.7 1.6 multiply_reduce_fusion
  135.7 1.2 reduce-window.11
  138.5 2.3 %copy-done.2 = bf16[2,1536,768]{2,1,0:T(8,128)(2,1)S(1)} copy-done((bf16[2,1536,768]{2,1,0:T(8,128)(2,1)S(1)}, bf16[2,1536,768]{2,1,0:T(8,128)(2,1)}, u32[]{:S(2)}) %copy-start.2) | copy-done | bytes 4718616
  140.8 2.3 %copy-done.3 = bf16[2,1536,768]{2,1,0:T(8,128)(2,1)S(1)} copy-done((bf16[2,1536,768]{2,1,0:T(8,128)(2,1)S(1)}, bf16[2,1536,768]{2,1,0:T(8,128)(2,1)}, u32[]{:S(2)}) %copy-start.3) | copy-done | bytes 4718616
  143.1 46.5 %run_experts.1 = bf16[8,80,1536]{2,1,0:T(8,128)(2,1)S(1)} custom-call(bf16[8,80,1536]{2,1,0:T(8,128)(2,1)S(1)} %bitcast.179, bf16[2,1536,768]{2,1,0:T(8,128)(2,1)S(1)} %copy-done.2, bf16[2,1536,768]{2,1,0:T(8,128)(2,1)S(1)} %copy-done.3, bf16[2,768,1536]{2,1,0:T(8,128)(2,1)} %down_ref.1), custom_call_target="tpu_custom_call" | custom-call | tf_op jit(solution)/shard_map/run_experts/pallas_call | solution.py:533
  190.7 1.2 fusion.12
  (104 shorter events, 11.6 us)
Async XLA Ops:
  0.0 189.6 %copy-start = (bf16[1536,16]{0,1:T(8,128)(2,1)S(1)}, bf16[1536,16]{0,1:T(8,128)(2,1)}, u32[]{:S(2)}) copy-start(bf16[1536,16]{0,1:T(8,128)(2,1)} %param.24) | copy-start | bytes 147460
  0.0 5.4 %copy-start.13 = (bf16[4,16,2048]{2,1,0:T(8,128)(2,1)S(1)}, bf16[4,16,2048]{2,1,0:T(8,128)(2,1)}, u32[]{:S(2)}) copy-start(bf16[4,16,2048]{2,1,0:T(8,128)(2,1)} %param.26) | copy-start | bytes 786436
  3.2 2.5 %copy-start.5 = (bf16[384,256]{1,0:T(8,128)(2,1)S(1)}, bf16[384,256]{1,0:T(8,128)(2,1)}, u32[]{:S(2)}) copy-start(bf16[384,256]{1,0:T(8,128)(2,1)} %proj_ref.1) | copy-start | bytes 589828
  5.0 79.3 %copy-start.17 = (s32[4,4]{1,0:T(4,128)S(1)}, s32[4,4]{1,0:T(4,128)}, u32[]{:S(2)}) copy-start(s32[4,4]{1,0:T(4,128)} %param.17) | copy-start | bytes 196
  5.0 81.3 %copy-start.15 = (bf16[1536]{0:T(1024)(128)(2,1)S(1)}, bf16[1536]{0:T(1024)(128)(2,1)}, u32[]{:S(2)}) copy-start(bf16[1536]{0:T(1024)(128)(2,1)} %param.20) | copy-start | bytes 9220
  5.0 81.3 %copy-start.6 = (bf16[128,1536]{1,0:T(8,128)(2,1)S(1)}, bf16[128,1536]{1,0:T(8,128)(2,1)}, u32[]{:S(2)}) copy-start(bf16[128,1536]{1,0:T(8,128)(2,1)} %param.16) | copy-start | bytes 1179652
  79.4 2.7 %copy-start.1 = (bf16[1536,2048]{1,0:T(8,128)(2,1)}, bf16[1536,2048]{1,0:T(8,128)(2,1)S(1)}, u32[]{:S(2)}) copy-start(bf16[1536,2048]{1,0:T(8,128)(2,1)S(1)} %get-tuple-element.8) | copy-start | bytes 18874372
  82.1 2.2 %copy-start.4 = (bf16[2304,1024]{1,0:T(8,128)(2,1)}, bf16[2304,1024]{1,0:T(8,128)(2,1)S(1)}, u32[]{:S(2)}) copy-start(bf16[2304,1024]{1,0:T(8,128)(2,1)S(1)} %get-tuple-element.10) | copy-start | bytes 14155780
  90.4 3.7 %copy-start.11 = (bf16[4,2,2,8,3328]{4,3,1,2,0:T(8,128)(2,1)}, bf16[4,2,2,8,3328]{4,3,1,2,0:T(8,128)(2,1)S(1)}, u32[]{:S(2)}) copy-start(bf16[4,2,2,8,3328]{4,3,1,2,0:T(8,128)(2,1)S(1)} %copy.143) | copy-start | bytes 2555908
  94.6 15.0 %copy-start.12 = (pred[768,1024]{1,0:T(8,128)(4,1)S(1)}, pred[768,1024]{1,0:T(8,128)(4,1)}, u32[]{:S(2)}) copy-start(pred[768,1024]{1,0:T(8,128)(4,1)} %fusion.4) | copy-start | bytes 2359300
  114.2 4.6 %copy-start.8 = (f32[2,768,1024]{2,1,0:T(8,128)S(1)}, f32[2,768,1024]{2,1,0:T(8,128)}, u32[]{:S(2)}) copy-start(f32[2,768,1024]{2,1,0:T(8,128)} %get-tuple-element.46) | copy-start | bytes 18874372
  120.8 4.5 %copy-start.9 = (bf16[2,6,128,128]{2,3,1,0:T(8,128)(2,1)}, bf16[2,6,128,128]{2,3,1,0:T(8,128)(2,1)S(1)}, u32[]{:S(2)}) copy-start(bf16[2,6,128,128]{2,3,1,0:T(8,128)(2,1)S(1)} %copy.117) | copy-start | bytes 1179652
  130.3 3.4 %copy-start.7 = (bf16[128,1536]{1,0:T(8,128)(2,1)S(1)}, bf16[128,1536]{1,0:T(8,128)(2,1)}, u32[]{:S(2)}) copy-start(bf16[128,1536]{1,0:T(8,128)(2,1)} %param.16) | copy-start | bytes 1179652
  130.3 3.4 %copy-start.10 = (bf16[2,6,128,128]{2,3,1,0:T(8,128)(2,1)S(1)}, bf16[2,6,128,128]{2,3,1,0:T(8,128)(2,1)}, u32[]{:S(2)}) copy-start(bf16[2,6,128,128]{2,3,1,0:T(8,128)(2,1)} %copy-done.9) | copy-start | bytes 1179652
  133.3 2.0 %copy-start.14 = (s32[128,4]{0,1:T(4,128)S(1)}, s32[128,4]{0,1:T(4,128)}, u32[]{:S(2)}) copy-start(s32[128,4]{0,1:T(4,128)} %param.19) | copy-start | bytes 6148
  133.3 4.3 %copy-start.16 = (bf16[1536]{0:T(1024)(128)(2,1)S(1)}, bf16[1536]{0:T(1024)(128)(2,1)}, u32[]{:S(2)}) copy-start(bf16[1536]{0:T(1024)(128)(2,1)} %param.21) | copy-start | bytes 9220
  138.4 2.3 %copy-start.2 = (bf16[2,1536,768]{2,1,0:T(8,128)(2,1)S(1)}, bf16[2,1536,768]{2,1,0:T(8,128)(2,1)}, u32[]{:S(2)}) copy-start(bf16[2,1536,768]{2,1,0:T(8,128)(2,1)} %gate_ref.1) | copy-start | bytes 14155780
  140.8 2.3 %copy-start.3 = (bf16[2,1536,768]{2,1,0:T(8,128)(2,1)S(1)}, bf16[2,1536,768]{2,1,0:T(8,128)(2,1)}, u32[]{:S(2)}) copy-start(bf16[2,1536,768]{2,1,0:T(8,128)(2,1)} %up_ref.1) | copy-start | bytes 14155780

commit v3 on v2

--- a/solution.py
+++ b/solution.py
@@ -259,10 +259,11 @@
         here = place(which, block_row, chip_d * 2 + core)
         to_pair(which, s, 3, here, here)
 
-    steps = [(which, s) for which in range(2) for s in range(rows)]
+    steps = [(0, 0), (1, 0)]
+    steps += [(which, s) for which in range(2) for s in range(1, rows)]
     for i, step in enumerate(steps):
         spread(*step)
-        if i == 0:
+        if i == 2:
             total = maps_ref[col].astype(jnp.float32)
             for s in range(1, columns):
                 part_copies[s - 1].wait_recv()
@@ -283,6 +284,7 @@
                 )
             mine = pltpu.make_async_copy(chunk, all_maps.at[col], own_sem.at[2])
             mine.start()
+        if i == 1:
             start_line(1)
         if i >= 1:
             relay(*steps[i - 1])
@@ -549,10 +551,40 @@
             dma((columns,)),
         ],
         compiler_params=pltpu.CompilerParams(
-            collective_id=2, has_side_effects=True, vmem_limit_bytes=40 * 1024 * 1024
+            collective_id=2, has_side_effects=True, vmem_limit_bytes=58 * 1024 * 1024
         ),
         name="run_experts",
     )(sending, gate, up, down)
+
+
+def project_kernel(rows, attended_ref, packed_ref, parts_ref):
+    depth = attended_ref.shape[1] // rows
+    tall = packed_ref.shape[0] // rows
+    half = depth // 2
+    attended = attended_ref[...]
+    sums = [None, None, None]
+    for r in range(rows):
+        mine = attended[:, r * depth : (r + 1) * depth]
+        front = packed_ref[r * tall : r * tall + depth, :]
+        side = packed_ref[r * tall + depth : (r + 1) * tall, :]
+        pairs = ((mine, front), (mine[:, :half], side), (mine[:, half:], side))
+        for i, (left, right) in enumerate(pairs):
+            term = jnp.dot(left, right, preferred_element_type=jnp.float32)
+            sums[i] = term if sums[i] is None else sums[i] + term
+    for i in range(3):
+        parts_ref[i] = sums[i]
+
+
+def project_out(attended, packed, rows):
+    vmem = pl.BlockSpec(memory_space=pltpu.VMEM)
+    return pl.pallas_call(
+        functools.partial(project_kernel, rows),
+        out_shape=jax.ShapeDtypeStruct((3, attended.shape[0], packed.shape[1]), jnp.float32),
+        in_specs=[vmem, vmem],
+        out_specs=vmem,
+        compiler_params=pltpu.CompilerParams(vmem_limit_bytes=24 * 1024 * 1024),
+        name="project_out",
+    )(attended, packed)
 
 
 def local(
@@ -693,23 +725,11 @@
     )
     row_count = lax.axis_size("row")
     if paired:
-        stacked = out_packed.reshape(row_count, packed.shape[0], columns * 128)
-        attended_parts = attention_result.reshape(token_rows, row_count, out_depth)
-        front = jnp.einsum(
-            "trk,rkn->tn",
-            attended_parts,
-            stacked[:, :out_depth],
-            preferred_element_type=jnp.float32,
-        ).reshape(token_rows, columns, 128)
-        halves = [
-            jnp.einsum(
-                "trk,rkn->tn",
-                attended_parts[:, :, h * (out_depth // 2) : (h + 1) * (out_depth // 2)],
-                stacked[:, out_depth:],
-                preferred_element_type=jnp.float32,
-            ).reshape(token_rows, columns, 128)[:, :, h * 64 : (h + 1) * 64]
-            for h in range(2)
-        ]
+        parts = project_out(attention_result, out_packed, row_count).reshape(
+            3, token_rows, columns, 128
+        )
+        front = parts[0]
+        halves = [parts[1][:, :, :64], parts[2][:, :, 64:]]
         projected_rows = jnp.concatenate([front, halves[0] + halves[1]], axis=2)
     else:
         projected_rows = jnp.dot(

time: 193 us -> 176 us (0.912)
  local copies, waits for them, and re-layouts: 22.5 us -> 11.7 us
  matrix products: 22.2 us -> 13.9 us
  Pallas kernels: 134 us -> 137 us
    dot_general x3 -> x0, matrix products: 7.47 us -> none  [the longest x2 4.42 us: local(): jnp.einsum('trk,rkn->tn', attended_parts[:, :, h * (out_depth // 2):(h +...]
    unnamed x43 -> x37, local copies, waits for them, and re-layouts: 11 us -> 5.8 us
    dot_general x2 -> x0, local copies, waits for them, and re-layouts: 5.01 us -> none  [local(): jnp.einsum('trk,rkn->tn', attended_parts, stacked[:, :out_depth], preferr...]
    dot_general x1, matrix products: 3.82 us -> 1.07 us  [local(): jnp.dot(normalized, qkv_full, preferred_element_type=jnp.float32)]
    dot_general x1, matrix products: 4.09 us -> 1.53 us  [local(): jnp.einsum('hqd,hkd->hqk', grouped, key_lines, preferred_element_type=jnp...]
    dot_general x1, matrix products: 1.62 us -> 4.16 us  [local(): jnp.einsum('hqk,hkd->hqd', weights.astype(jnp.bfloat16), value_lines, pre...]
    slice x2, local copies, waits for them, and re-layouts: 2.33 us -> 0.32 us  [local(): projection_all[:, :QUERY_HEADS * HEAD_SIZE]]
where the time goes in v3:
time: 176 us; the launch traced here: 175 us
  Pallas kernels  137 us (78%)
  matrix products  13.9 us (8%)
  other arithmetic  12.6 us (7%)
  local copies, waits for them, and re-layouts  11.7 us (7%)
    pallas_call x1, Pallas kernels, gather_weights(): pl.pallas_call(functools.partial(gather_kernel, rows, columns), out_shape...  74 us
    pallas_call x1, Pallas kernels, run_experts(): pl.pallas_call(functools.partial(experts_kernel, columns), out_shape=jax....  47.5 us
    pallas_call x1, Pallas kernels, share(): pl.pallas_call(functools.partial(share_kernel, columns, exchange), out_sh...  13.9 us
    unnamed x37, local copies, waits for them, and re-layouts  5.8 us
    dot_general x1, matrix products, local(): jnp.einsum('hqk,hkd->hqd', weights.astype(jnp.bfloat16), value_lines, pre...  4.16 us

profile of v3, /device:TPU:1, one launch (start us, length us, event | category | flops | bytes accessed | tf_op | source)
XLA Modules:
  0.0 175.4 jit_solution(16467947044477758975)
XLA Ops:
  0.0 0.7 compare_bitcast_fusion.3
  0.8 1.1 bitcast_convert_fusion.7
  1.9 0.9 bitcast_convert_fusion.15
  4.1 74.0 %gather_weights.1 = (bf16[1536,2048]{1,0:T(8,128)(2,1)S(1)}, bf16[2304,1024]{1,0:T(8,128)(2,1)S(1)}, bf16[8,16,3328]{2,1,0:T(8,128)(2,1)S(1)}) custom-call(bf16[384,256]{1,0:T(8,128)(2,1)S(1)} %copy-done.3, bf16[576,128]{1,0:T(8,128)(2,1)S(1)} %maximum_maximum_fusion.out_ref, bf16[8,16,3328]{2,1,0:T(8,128)(2,1)S(1)} %bitcast.157), custom_call_target="tpu_custom_call" | custom-call | tf_op jit(solution)/shard_map/gather_weights/pallas_call | solution.py:313
  78.1 2.2 %copy-done.1 = bf16[2304,1024]{1,0:T(8,128)(2,1)} copy-done((bf16[2304,1024]{1,0:T(8,128)(2,1)}, bf16[2304,1024]{1,0:T(8,128)(2,1)S(1)}, u32[]{:S(2)}) %copy-start.1) | copy-done | bytes 4718616
  80.5 1.1 fusion.41
  81.9 0.8 fusion.11
  83.9 13.9 %share.1 = bf16[8,128,512]{2,1,0:T(8,128)(2,1)S(1)} custom-call(bf16[128,512]{1,0:T(8,128)(2,1)S(1)} %pad_maximum_fusion.4.block_ref), custom_call_target="tpu_custom_call" | custom-call | tf_op jit(solution)/shard_map/share/pallas_call | solution.py:379
  97.8 0.9 fusion.62
  98.9 1.0 copy.105
  100.7 0.8 fusion.4
  101.5 1.5 select_reduce_fusion
  103.1 2.3 %fusion = f32[2,768]{1,0:T(2,128)S(1)} fusion(f32[2,768,1024]{2,1,0:T(8,128)S(1)} %get-tuple-element.49, f32[2,768]{1,0:T(2,128)S(1)} %broadcast_maximum_fusion, pred[768,1024]{1,0:T(8,128)(4,1)S(1)} %fusion.4), kind=kLoop, calls=%fused_computation.2 | loop fusion | flops 6289920 | bytes 7090176 | tf_op jit(solution)/shard_map/reduce_sum | solution.py:712
  106.2 4.2 %fusion.21 = bf16[2,768,128]{2,1,0:T(8,128)(2,1)S(1)} fusion(f32[2,768,1024]{2,1,0:T(8,128)} %copy-done.6, f32[2,768]{1,0:T(2,128)S(1)} %broadcast_maximum_fusion, pred[768,1024]{1,0:T(8,128)(4,1)S(1)} %fusion.4, bf16[1024,2,128]{2,0,1:T(8,128)(2,1)S(1)} %copy.107, f32[2,768]{1,0:T(2,128)S(1)} %fusion), kind=kOutput, calls=%fused_computation.31 | convolution fusion | flops 409337856 | bytes 8007680 | tf_op jit(solution)/shard_map/hqk,hkd->hqd/dot_general | solution.py:713
  110.8 2.3 %copy-done.2 = bf16[2304,1024]{1,0:T(8,128)(2,1)S(1)} copy-done((bf16[2304,1024]{1,0:T(8,128)(2,1)S(1)}, bf16[2304,1024]{1,0:T(8,128)(2,1)}, u32[]{:S(2)}) %copy-start.2) | copy-done | bytes 4718616
  113.2 1.3 project_out.1
  114.5 1.0 copy.119
  115.7 1.7 slice_add_fusion
  117.6 1.0 pad_maximum_fusion.3
  120.2 1.2 reduce-window.11
  122.5 2.0 %convolution_convert_fusion = bf16[640,1536]{1,0:T(8,128)(2,1)} fusion(pred[128,640]{1,0:T(8,128)(4,1)S(1)} %fusion.15, f32[128,1536]{1,0:T(8,128)S(1)} %get-tuple-element.51, f32[1536]{0:T(1024)S(1)} %convert_element_type.136, f32[128]{0:T(128)S(1)} %add_rsqrt_fusion), kind=kOutput, calls=%fused_computation.4 | convolution fusion | flops 253231104 | bytes 2841088 | tf_op jit(solution)/shard_map/tj,td->jd/dot_general | solution.py:764
  124.5 47.5 %run_experts.1 = bf16[8,80,1536]{2,1,0:T(8,128)(2,1)} custom-call(bf16[8,80,1536]{2,1,0:T(8,128)(2,1)} %bitcast.161, bf16[2,1536,768]{2,1,0:T(8,128)(2,1)} %gate_ref.1, bf16[2,1536,768]{2,1,0:T(8,128)(2,1)} %up_ref.1, bf16[2,768,1536]{2,1,0:T(8,128)(2,1)} %down_ref.1), custom_call_target="tpu_custom_call" | custom-call | tf_op jit(solution)/shard_map/run_experts/pallas_call | solution.py:535
  172.1 2.2 %fusion.44 = f32[128,1536]{1,0:T(8,128)S(1)} fusion(bf16[640,1536]{1,0:T(8,128)(2,1)} %bitcast.159, f32[128,640]{1,0:T(8,128)S(1)} %select_reduce_fusion.1), kind=kOutput, calls=%fused_computation.66 | convolution fusion | flops 251740160 | bytes 3080192 | tf_op jit(solution)/shard_map/dot_general | solution.py:774
  174.2 1.2 fusion.12
  (100 shorter events, 8.1 us)
Async XLA Ops:
  0.0 119.6 %copy-start = (bf16[1536,16]{0,1:T(8,128)(2,1)S(1)}, bf16[1536,16]{0,1:T(8,128)(2,1)}, u32[]{:S(2)}) copy-start(bf16[1536,16]{0,1:T(8,128)(2,1)} %param.24) | copy-start | bytes 147460
  0.0 3.2 %copy-start.10 = (bf16[4,16,2048]{2,1,0:T(8,128)(2,1)S(1)}, bf16[4,16,2048]{2,1,0:T(8,128)(2,1)}, u32[]{:S(2)}) copy-start(bf16[4,16,2048]{2,1,0:T(8,128)(2,1)} %param.26) | copy-start | bytes 786436
  0.7 2.8 %copy-start.9 = (bf16[384,192]{0,1:T(8,128)(2,1)S(1)}, bf16[384,192]{0,1:T(8,128)(2,1)}, u32[]{:S(2)}) copy-start(bf16[384,192]{0,1:T(8,128)(2,1)} %param.23) | copy-start | bytes 442372
  1.8 2.0 %slice-start = ((bf16[384,192]{0,1:T(8,128)(2,1)}), bf16[384,128]{0,1:T(8,128)(2,1)S(1)}, s32[]{:S(2)}) async-start(bf16[384,192]{0,1:T(8,128)(2,1)} %param.23), calls=%async_computation | async-start | bytes 196608 | tf_op jit(solution)/shard_map/slice | solution.py:651
  2.8 1.3 copy-start.3
  3.2 77.1 %copy-start.12 = (bf16[1536]{0:T(1024)(128)(2,1)S(1)}, bf16[1536]{0:T(1024)(128)(2,1)}, u32[]{:S(2)}) copy-start(bf16[1536]{0:T(1024)(128)(2,1)} %param.20) | copy-start | bytes 9220
  3.2 77.1 %copy-start.5 = (bf16[128,1536]{1,0:T(8,128)(2,1)S(1)}, bf16[128,1536]{1,0:T(8,128)(2,1)}, u32[]{:S(2)}) copy-start(bf16[128,1536]{1,0:T(8,128)(2,1)} %param.16) | copy-start | bytes 1179652
  78.1 2.2 %copy-start.1 = (bf16[2304,1024]{1,0:T(8,128)(2,1)}, bf16[2304,1024]{1,0:T(8,128)(2,1)S(1)}, u32[]{:S(2)}) copy-start(bf16[2304,1024]{1,0:T(8,128)(2,1)S(1)} %get-tuple-element.10.packed_ref) | copy-start | bytes 14155780
  80.5 1.2 copy-start.14
  100.2 1.3 copy-start.8
  103.1 2.7 %copy-start.6 = (f32[2,768,1024]{2,1,0:T(8,128)}, f32[2,768,1024]{2,1,0:T(8,128)S(1)}, u32[]{:S(2)}) copy-start(f32[2,768,1024]{2,1,0:T(8,128)S(1)} %get-tuple-element.49) | copy-start | bytes 18874372
  103.1 2.6 %copy-start.7 = (bf16[1024,256]{1,0:T(8,128)(2,1)S(1)}, bf16[1024,256]{1,0:T(8,128)(2,1)}, u32[]{:S(2)}) copy-start(bf16[1024,256]{1,0:T(8,128)(2,1)} %get-tuple-element.16) | copy-start | bytes 1572868
  110.8 2.3 %copy-start.2 = (bf16[2304,1024]{1,0:T(8,128)(2,1)S(1)}, bf16[2304,1024]{1,0:T(8,128)(2,1)}, u32[]{:S(2)}) copy-start(bf16[2304,1024]{1,0:T(8,128)(2,1)} %copy-done.1) | copy-start | bytes 14155780
  117.6 1.9 %copy-start.13 = (bf16[1536]{0:T(1024)(128)(2,1)S(1)}, bf16[1536]{0:T(1024)(128)(2,1)}, u32[]{:S(2)}) copy-start(bf16[1536]{0:T(1024)(128)(2,1)} %param.21) | copy-start | bytes 9220
  117.6 2.2 %copy-start.11 = (s32[128,4]{0,1:T(4,128)S(1)}, s32[128,4]{0,1:T(4,128)}, u32[]{:S(2)}) copy-start(s32[128,4]{0,1:T(4,128)} %param.19) | copy-start | bytes 6148
  172.0 2.2 %copy-start.4 = (bf16[8,80,1536]{2,1,0:T(8,128)(2,1)S(1)}, bf16[8,80,1536]{2,1,0:T(8,128)(2,1)}, u32[]{:S(2)}) copy-start(bf16[8,80,1536]{2,1,0:T(8,128)(2,1)} %run_experts.1) | copy-start | bytes 5898244
